TPU v7x, 32 devices: a whole 2x2x4 slice. The times are simulated.
32 devices in a mesh: groups: 2 (over y), heads: 4 (over x, core), tm: 4 (over z).
Axes of the slice: x: 2, y: 2, z: 4, core: 2. Of those that a mesh axis runs over, the one named last changes fastest.
Arguments:
- queries: bfloat16 [256, 8192], P('groups', 'heads'), parts along dimension 0, may hold values from -6 to 6
- cache_keys: bfloat16 [8192, 8192], P(('groups', 'tm'), 'heads'), parts along dimension 0, may hold values from -650 to 650
- cache_values: bfloat16 [8192, 8192], P(('groups', 'tm'), 'heads'), parts along dimension 0, may hold values from -6 to 6
- residual: bfloat16 [256, 8192], P('groups', 'tm'), parts along dimension 0, may hold values from -20 to 20
- out_weight: bfloat16 [8192, 8192], P('heads', 'tm'), may hold values from -0.0625 to 0.0625
- norm_gain: float32 [8192], P('tm'), may hold values from 0.1 to 1.9
- cond_weight: bfloat16 [8192, 1536], P('tm', 'heads'), may hold values from -0.0625 to 0.0625
- in_weight: bfloat16 [1152, 1536], replicated, may hold values from -0.1875 to 0.1875
- head_out: bfloat16 [1536, 1152], replicated, may hold values from -0.15625 to 0.15625
- start_state: float32 [256, 1152], P(('groups', 'heads')), parts along dimension 0, may hold values from -6 to 6
- noise_draws: bfloat16 [256, 8, 1152], P(('groups', 'heads'), 'tm'), parts along dimension 0, may hold values from -6 to 6
- positions: int32 [256], P('groups'), parts along dimension 0, may hold values from 0 to 4095
- cache_length: int32 [2], P('groups'), parts along dimension 0, may hold values from 2048 to 4096
- plan: int32 [9], replicated, may hold values from 0 to 1000, as said below
Outputs:
- states: float32 [256, 8, 1152], P(('groups', 'heads'), 'tm'), parts along dimension 0
There are 2 independent parts, one for each index of `groups`. A program takes and returns all parts, laid end to end along the dimension named above; an argument that names none is the same for every part. Nothing has to cross between parts.
Inputs may be any that keep to these rules, and one draw needn't show every extreme that they name: `plan`: strictly decreasing; the first entry is 1000 and the last is 0.
All inputs are finite; a program needn't handle non-finite values.
Results may differ from a plain program's by a relative error of at most 0.0028.
Values may be sent and summed in bfloat16 or wider, within the bound.
A program may use at most 128 MiB of HBM per device.

v0:
```python
import math

import jax
import jax.numpy as jnp
from jax import lax
from jax.sharding import PartitionSpec as P

D = 8192
HD = 128
WIDTH = 1536
CHAN = 1152
SWEEPS = 3


def merged(part, axis, combine):
    gathered = jax.tree.map(lambda a: lax.all_gather(a, axis), part)

    def take(source):
        return jax.tree.map(lambda a: lax.dynamic_index_in_dim(a, source, 0, False), gathered)

    return lax.fori_loop(
        1, lax.axis_size(axis), lambda source, state: combine(state, take(source)), take(0)
    )


def rotate(values, angle_pos):
    head_feature_width = values.shape[-1]
    half_dim = head_feature_width // 2
    frequencies = jnp.exp(
        -math.log(10000.0) * 2.0 * jnp.arange(half_dim, dtype=jnp.float32) / head_feature_width
    )
    angles = angle_pos[:, None] * frequencies[None, :]
    cosine = jnp.cos(angles)[:, None, :]
    sine_part = jnp.sin(angles)[:, None, :]
    paired = values.astype(jnp.float32).reshape(values.shape[0], values.shape[1], half_dim, 2)
    real_part = paired[..., 0]
    imag_part = paired[..., 1]
    turned = jnp.stack(
        [real_part * cosine - imag_part * sine_part, real_part * sine_part + imag_part * cosine],
        axis=-1,
    )
    return turned.reshape(values.shape).astype(jnp.bfloat16)


def time_terms(levels, hidden_width):
    half_width = hidden_width // 2
    frequencies = jnp.exp(
        -math.log(10000.0) * jnp.arange(half_width, dtype=jnp.float32) / half_width
    )
    angles = levels[:-1, None] * frequencies[None, :]
    embedding = jnp.concatenate([jnp.sin(angles), jnp.cos(angles)], axis=1)
    step_size = (levels[:-1] - levels[1:]) / 1000.0
    return (embedding, step_size, jnp.sqrt(step_size))


def block_attend(rotary_applied, block_key_rows, block_value_rows, valid_keys):
    head_feature_width = rotary_applied.shape[-1]
    attention_logits = jnp.einsum(
        "orp,brp->orb", rotary_applied, block_key_rows, preferred_element_type=jnp.float32
    ) * (1.0 / math.sqrt(head_feature_width))
    masked = jnp.where(valid_keys[None, None, :], attention_logits, jnp.float32(-1e30))
    block_max = jnp.max(masked, axis=2)
    weights = jnp.where(
        valid_keys[None, None, :], jnp.exp(masked - block_max[:, :, None]), jnp.float32(0.0)
    )
    block_total = jnp.sum(weights, axis=2)
    block_output_part = jnp.einsum(
        "pzu,uzx->pzx",
        weights.astype(jnp.bfloat16),
        block_value_rows,
        preferred_element_type=jnp.float32,
    )
    return (block_max, block_total, block_output_part)


def combine(earlier, latter):
    max_one, total_one, out_one = earlier
    max_two, total_two, out_two = latter
    highest = jnp.maximum(max_one, max_two)
    scale_one = jnp.exp(max_one - highest)
    scale_two = jnp.exp(max_two - highest)
    merged_total = total_one * scale_one + total_two * scale_two
    merged_out = out_one * scale_one[:, :, None] + out_two * scale_two[:, :, None]
    return (highest, merged_total, merged_out)


def prefix_sum(totals):
    gathered = lax.all_gather(totals[None], "tm", axis=0, tiled=True)
    lower_mask = (jnp.arange(gathered.shape[0], dtype=jnp.int32) < lax.axis_index("tm")).astype(
        jnp.float32
    )
    return jnp.sum(gathered * lower_mask[:, None, None], axis=0)


def shards(
    queries,
    cache_keys,
    cache_values,
    residual,
    out_weight,
    norm_gain,
    cond_weight,
    in_weight,
    head_out,
    start_state,
    noise_draws,
    positions,
    cache_length,
    plan,
):
    row_total = queries.shape[0]
    local_heads = queries.shape[1] // HD
    key_count = cache_keys.shape[0]
    time_index = lax.axis_index("tm")
    head_index = lax.axis_index("heads")
    rotary_applied = rotate(
        queries.reshape(row_total, local_heads, HD), positions.astype(jnp.float32)
    )
    key_pos = time_index * key_count + jnp.arange(key_count, dtype=jnp.int32)
    valid_keys = key_pos < cache_length[0]
    partial_value = block_attend(
        rotary_applied,
        cache_keys.reshape(key_count, local_heads, HD),
        cache_values.reshape(key_count, local_heads, HD),
        valid_keys,
    )
    merged_max, merged_total, merged_out = merged(partial_value, "tm", combine)
    attended = (
        (merged_out / merged_total[:, :, None])
        .reshape(row_total, local_heads * HD)
        .astype(jnp.bfloat16)
    )
    row_each = start_state.shape[0]
    first_row = head_index * row_each
    projected = lax.psum(jnp.dot(attended, out_weight, preferred_element_type=jnp.float32), "heads")
    hidden = residual.astype(jnp.float32) + projected
    hidden_rows = lax.dynamic_slice_in_dim(hidden, first_row, row_each, 0)
    squares = jnp.sum(hidden_rows * hidden_rows, axis=1)
    scaled = (hidden * norm_gain[None, :]).astype(jnp.bfloat16)
    cond_part = jnp.dot(scaled, cond_weight, preferred_element_type=jnp.float32)
    square_sum, cond_sum = lax.psum((squares, cond_part), "tm")
    inverse = lax.rsqrt(square_sum / D + 1e-06)
    condition = (
        lax.all_to_all(cond_sum, "heads", split_axis=0, concat_axis=1, tiled=True)
        * inverse[:, None]
    )
    time_each = noise_draws.shape[1]
    levels = lax.dynamic_slice_in_dim(plan, time_index * time_each, time_each + 1, 0).astype(
        jnp.float32
    )
    embedding, step_size, noise_scale = time_terms(levels, in_weight.shape[1])
    noise_term = noise_scale[None, :, None] * noise_draws.astype(jnp.float32)
    states = jnp.broadcast_to(start_state[:, None, :], noise_draws.shape)
    for sweep_index in range(SWEEPS):
        flat_states = states.astype(jnp.bfloat16).reshape(row_each * time_each, CHAN)
        preact = jnp.dot(flat_states, in_weight, preferred_element_type=jnp.float32).reshape(
            row_each, time_each, WIDTH
        )
        preact = preact + condition[:, None, :] + embedding[None]
        action = jax.nn.silu(preact).astype(jnp.bfloat16)
        drift_term = jnp.dot(
            action.reshape(row_each * time_each, WIDTH),
            head_out,
            preferred_element_type=jnp.float32,
        ).reshape(row_each, time_each, CHAN)
        increment = step_size[None, :, None] * drift_term + noise_term
        running = jnp.cumsum(increment, axis=1)
        before = prefix_sum(running[:, -1, :])
        states = start_state[:, None, :] + before[:, None, :] + (running - increment)
    return states


def solution(mesh):
    placed = (
        P("groups", "heads"),
        P(("groups", "tm"), "heads"),
        P(("groups", "tm"), "heads"),
        P("groups", "tm"),
        P("heads", "tm"),
        P("tm"),
        P("tm", "heads"),
        P(),
        P(),
        P(("groups", "heads"), None),
        P(("groups", "heads"), "tm", None),
        P("groups"),
        P("groups"),
        P(),
    )
    return jax.shard_map(
        shards,
        mesh=mesh,
        in_specs=placed,
        out_specs=P(("groups", "heads"), "tm", None),
        check_vma=False,
    )
```

profile of v0, /device:TPU:0, one launch (start us, length us, event | category | flops | bytes accessed | tf_op | source)
XLA Modules:
  0.0 314.7 jit_solution(7323992095895758402)
XLA Ops:
  8.2 2.1 copy.29
  10.3 2.5 convert.9
  12.9 2.9 subtract_convert_fusion
  15.8 1.2 pad_maximum_fusion
  17.1 4.3 %bitcast_reduce_fusion = (f32[128,16]{0,1:T(8,128)S(1)}, f32[16,128,1024]{2,1,0:T(8,128)S(1)}) fusion(pred[1024]{0:T(1024)(128)(4,1)S(1)} %add_compare_fusion, bf16[128,16,128]{0,2,1:T(8,128)(2,1)S(1)} %bitcast.134, bf16[1024,2048]{1,0:T(8,128)(2,1)} %param.17), kind=kOutput, calls=%fused_computation.10 | convolution fusion | flops 543160320 | bytes 13116416 | tf_op jit(solution)/shard_map/orp,brp->orb/dot_general | solution.py:58
  21.4 3.2 %copy-done.1 = f32[16,128,1024]{2,1,0:T(8,128)} copy-done((f32[16,128,1024]{2,1,0:T(8,128)}, f32[16,128,1024]{2,1,0:T(8,128)S(1)}, u32[]{:S(2)}) %copy-start.1) | copy-done | bytes 8388632
  24.6 3.5 %fusion.67 = f32[128,16,128]{2,0,1:T(8,128)} fusion(f32[16,128,1024]{2,1,0:T(8,128)S(1)} %get-tuple-element.228, f32[128,16]{0,1:T(8,128)S(1)} %get-tuple-element.227, pred[1024]{0:T(1024)(128)(4,1)S(1)} %add_compare_fusion, bf16[1024,2048]{1,0:T(8,128)(2,1)S(1)} %copy-done.9), kind=kOutput, calls=%fused_computation.52 | convolution fusion | flops 547356672 | bytes 13640704 | tf_op jit(solution)/shard_map/pzu,uzx->pzx/dot_general | solution.py:67
  28.2 14.8 %all-gather = f32[512,16]{0,1:T(8,128)S(1)} all-gather(f32[128,16]{0,1:T(8,128)S(1)} %get-tuple-element.227), channel_id=2, replica_groups=mesh['groups'=2,'heads'=4,'tm'=4] {'tm'}, dimensions={0}, use_global_device_ids=true | all-gather | bytes 40960 | tf_op jit(solution)/shard_map/all_gather | solution.py:16
  44.2 1.4 reshape.142
  45.6 4.6 %fusion.5 = f32[128,16]{0,1:T(8,128)S(1)} fusion(f32[16,128,1024]{2,1,0:T(8,128)} %copy-done.1, f32[128,16]{0,1:T(8,128)S(1)} %get-tuple-element.227, pred[1024]{0:T(1024)(128)(4,1)S(1)} %add_compare_fusion), kind=kLoop, calls=%fused_computation.15 | loop fusion | flops 10483712 | bytes 8406016 | tf_op jit(solution)/shard_map/reduce_sum | solution.py:66
  50.2 13.3 %all-gather.1 = f32[512,16]{0,1:T(8,128)S(1)} all-gather(f32[128,16]{0,1:T(8,128)S(1)} %fusion.5), channel_id=3, replica_groups=mesh['groups'=2,'heads'=4,'tm'=4] {'tm'}, dimensions={0}, use_global_device_ids=true | all-gather | bytes 40960 | tf_op jit(solution)/shard_map/all_gather | solution.py:16
  64.8 1.4 reshape.143
  66.1 1.6 convert_element_type.64
  68.9 43.3 %all-gather.8.cloned.1.call-done = f32[512,16,128]{2,0,1:T(8,128)} async-done(((f32[128,16,128]{2,0,1:T(8,128)}), f32[512,16,128]{2,0,1:T(8,128)}) %all-gather.8.cloned.1.call-update) | async-done | bytes 4194320 | tf_op jit(solution)/shard_map/all_gather | solution.py:16
  112.2 1.3 slice.39
  113.5 1.6 copy.34
  115.1 24.9 %while.19 = (s32[]{:T(128)}, f32[128,16]{0,1:T(8,128)}, f32[128,16]{0,1:T(8,128)}, f32[128,16,128]{2,1,0:T(8,128)}, f32[4,128,16]{1,0,2:T(4,128)}, /*index=5*/f3...) while((s32[]{:T(128)}, f32[128,16]{0,1:T(8,128)}, ...), condition=%wide.region_3.4_spmd, body=%wide.region_2.3_spmd.sunk | while | flops 798725 | bytes 5390479 | solution.py:21
  115.9 1.3 multiply_add_fusion.2
  118.7 1.3 constant_dynamic-slice_fusion.6
  120.0 3.4 %fusion.123 = f32[128,16,128]{2,1,0:T(8,128)} fusion(f32[1,128,16,128]{3,1,0,2:T(8,128)S(1)} %constant_dynamic-slice_fusion.6, f32[128,16,128]{2,1,0:T(8,128)} %get-tuple-element.297, f32[128,16]{1,0:T(8,128)} %copy.79, f32[128,16]{1,0:T(8,128)} %copy.80), kind=kLoop, calls=%fused_computation.2.clone.1 | loop fusion | flops 786432 | bytes 3162112 | tf_op jit(solution)/shard_map/while/body/eval_jaxpr/add | solution.py:83
  124.2 1.3 multiply_add_fusion.2
  126.9 1.3 constant_dynamic-slice_fusion.6
  128.3 3.4 %fusion.123 = f32[128,16,128]{2,1,0:T(8,128)} fusion(f32[1,128,16,128]{3,1,0,2:T(8,128)S(1)} %constant_dynamic-slice_fusion.6, f32[128,16,128]{2,1,0:T(8,128)} %get-tuple-element.297, f32[128,16]{1,0:T(8,128)} %copy.79, f32[128,16]{1,0:T(8,128)} %copy.80), kind=kLoop, calls=%fused_computation.2.clone.1 | loop fusion | flops 786432 | bytes 3162112 | tf_op jit(solution)/shard_map/while/body/eval_jaxpr/add | solution.py:83
  132.5 1.3 multiply_add_fusion.2
  135.2 1.3 constant_dynamic-slice_fusion.6
  136.5 3.4 %fusion.123 = f32[128,16,128]{2,1,0:T(8,128)} fusion(f32[1,128,16,128]{3,1,0,2:T(8,128)S(1)} %constant_dynamic-slice_fusion.6, f32[128,16,128]{2,1,0:T(8,128)} %get-tuple-element.297, f32[128,16]{1,0:T(8,128)} %copy.79, f32[128,16]{1,0:T(8,128)} %copy.80), kind=kLoop, calls=%fused_computation.2.clone.1 | loop fusion | flops 786432 | bytes 3162112 | tf_op jit(solution)/shard_map/while/body/eval_jaxpr/add | solution.py:83
  139.9 1.4 copy.38
  141.4 1.6 divide_convert_fusion
  143.0 5.7 %fusion.73 = f32[128,2048]{1,0:T(8,128)} fusion(bf16[2048,2048]{1,0:T(8,128)(2,1)} %param.20, bf16[16,8,16,128]{3,2,1,0:T(8,128)(2,1)S(1)} %bitcast.130), kind=kOutput, calls=%fused_computation.60 | convolution fusion | flops 1073741824 | bytes 9961472 | tf_op jit(solution)/shard_map/dot_general | solution.py:135
  150.4 33.1 %all-reduce.3.cloned.1.call-done = f32[128,2048]{1,0:T(8,128)} async-done(((f32[128,2048]{1,0:T(8,128)}), f32[128,2048]{1,0:T(8,128)}) %all-reduce.3.cloned.1.call-update) | async-done | bytes 1048592 | tf_op jit(solution)/shard_map/psum | solution.py:135
  183.6 1.5 convert_add_fusion
  186.0 2.5 fusion.72
  189.3 1.6 multiply_reduce_fusion.3
  190.9 12.3 %psum.23 = f32[32]{0:T(128)} all-reduce(f32[32]{0:T(128)} %multiply_reduce_fusion.3), channel_id=1, replica_groups=mesh['groups'=2,'heads'=4,'tm'=4] {'tm'}, use_global_device_ids=true, to_apply=%region_7.8 | all-reduce | flops 32 | bytes 256 | tf_op jit(solution)/shard_map/psum | solution.py:141
  203.2 20.7 %all-reduce.5.cloned.1.call-done = f32[4,32,384]{2,1,0:T(8,128)} async-done(((f32[4,32,384]{2,1,0:T(8,128)}), f32[4,32,384]{2,1,0:T(8,128)}) %all-reduce.5.cloned.1.call-update) | async-done | bytes 196624 | tf_op jit(solution)/shard_map/psum | solution.py:141
  223.9 4.0 %all-to-all-start = ((f32[4,32,384]{2,1,0:T(8,128)}), f32[4,32,384]{2,1,0:T(8,128)}, u32[]{:S(2)}, u32[]{:S(2)}) async-start(f32[4,32,384]{2,1,0:T(8,128)} %all-reduce.5.cloned.1.call-done), calls=%async_computation | async-start | bytes 393216 | tf_op jit(solution)/shard_map/all_to_all | solution.py:144
  227.9 1.1 add_rsqrt_fusion
  229.0 4.3 %all-to-all-done = f32[4,32,384]{2,1,0:T(8,128)} async-done(((f32[4,32,384]{2,1,0:T(8,128)}), f32[4,32,384]{2,1,0:T(8,128)}, u32[]{:S(2)}, u32[]{:S(2)}) %all-to-all-start) | async-done | bytes 196640 | tf_op jit(solution)/shard_map/all_to_all | solution.py:144
  234.3 1.4 broadcast_multiply_fusion
  235.7 4.2 %fusion.46 = f32[32,2,1152]{2,0,1:T(8,128)} fusion(bf16[1536,1152]{1,0:T(8,128)(2,1)S(1)} %copy-done, bf16[1152,1536]{1,0:T(8,128)(2,1)} %param.23, f32[2,1536]{1,0:T(2,128)S(1)} %pad_maximum_fusion.1, f32[32,1536]{1,0:T(8,128)} %broadcast_multiply_fusion, f32[2]{0:T(128)S(1)} %get-tuple-element.216, f32[2]{0:T(128)} %get-tuple-element.217, ...), kind=kOutput, calls=%fused_computation.45 | convolution fusion | flops 453967872 | bytes 7802896 | tf_op jit(solution)/shard_map/dot_general | solution.py:161
  241.6 15.9 %all-gather.3 = f32[128,1,1152]{2,0,1:T(8,128)S(1)} all-gather(f32[32,1,1152]{2,0,1:T(8,128)S(1)} %slice.40), channel_id=5, replica_groups=mesh['groups'=2,'heads'=4,'tm'=4] {'tm'}, dimensions={0}, use_global_device_ids=true | all-gather | bytes 737280 | tf_op jit(solution)/shard_map/all_gather | solution.py:88
  258.3 1.6 add.204
  259.9 4.4 %fusion.43 = f32[32,2,1152]{2,0,1:T(8,128)} fusion(bf16[1536,1152]{1,0:T(8,128)(2,1)S(1)} %copy-done, bf16[1152,1536]{1,0:T(8,128)(2,1)} %param.23, f32[2,1536]{1,0:T(2,128)S(1)} %pad_maximum_fusion.1, f32[32,1536]{1,0:T(8,128)} %broadcast_multiply_fusion, f32[32,2,1152]{2,0,1:T(8,128)} %copy-done.4, f32[32,2,1152]{2,0,1:T(8,128)} %fusion.46, ...), kind=kOutput, calls=%fused_computation.44 | convolution fusion | flops 454189056 | bytes 8466448 | tf_op jit(solution)/shard_map/dot_general | solution.py:161
  265.9 15.5 %all-gather.4 = f32[128,1,1152]{2,0,1:T(8,128)S(1)} all-gather(f32[32,1,1152]{2,0,1:T(8,128)S(1)} %slice.41), channel_id=6, replica_groups=mesh['groups'=2,'heads'=4,'tm'=4] {'tm'}, dimensions={0}, use_global_device_ids=true | all-gather | bytes 737280 | tf_op jit(solution)/shard_map/all_gather | solution.py:88
  282.2 1.6 add.211
  283.8 4.4 %fusion.40 = f32[32,2,1152]{2,0,1:T(8,128)} fusion(bf16[1536,1152]{1,0:T(8,128)(2,1)S(1)} %copy-done, bf16[1152,1536]{1,0:T(8,128)(2,1)} %param.23, f32[2,1536]{1,0:T(2,128)S(1)} %pad_maximum_fusion.1, f32[32,1536]{1,0:T(8,128)} %broadcast_multiply_fusion, f32[32,2,1152]{2,0,1:T(8,128)} %copy-done.3, f32[32,2,1152]{2,0,1:T(8,128)} %fusion.43, ...), kind=kOutput, calls=%fused_computation.43 | convolution fusion | flops 454189056 | bytes 8466448 | tf_op jit(solution)/shard_map/dot_general | solution.py:161
  289.2 15.4 %all-gather.5 = f32[128,1,1152]{2,0,1:T(8,128)S(1)} all-gather(f32[32,1,1152]{2,0,1:T(8,128)S(1)} %slice.42), channel_id=7, replica_groups=mesh['groups'=2,'heads'=4,'tm'=4] {'tm'}, dimensions={0}, use_global_device_ids=true | all-gather | bytes 737280 | tf_op jit(solution)/shard_map/all_gather | solution.py:88
  306.2 1.0 subtract_add_fusion
  (60 shorter events, 24.5 us)
Async XLA Ops:
  6.5 229.1 %copy-start = (bf16[1536,1152]{1,0:T(8,128)(2,1)S(1)}, bf16[1536,1152]{1,0:T(8,128)(2,1)}, u32[]{:S(2)}) copy-start(bf16[1536,1152]{1,0:T(8,128)(2,1)} %param.24) | copy-start | bytes 10616836
  6.5 105.6 %all-gather.8.cloned.1.call-start = ((), (), s32[]{:S(2)}) async-start(), calls=%async_computation.3 | async-start | bytes 5242880 | tf_op jit(solution)/shard_map/all_gather | solution.py:16
  17.0 7.6 %copy-start.9 = (bf16[1024,2048]{1,0:T(8,128)(2,1)S(1)}, bf16[1024,2048]{1,0:T(8,128)(2,1)}, u32[]{:S(2)}) copy-start(bf16[1024,2048]{1,0:T(8,128)(2,1)} %param.18) | copy-start | bytes 12582916
  21.4 3.2 %copy-start.1 = (f32[16,128,1024]{2,1,0:T(8,128)}, f32[16,128,1024]{2,1,0:T(8,128)S(1)}, u32[]{:S(2)}) copy-start(f32[16,128,1024]{2,1,0:T(8,128)S(1)} %get-tuple-element.228) | copy-start | bytes 25165828
  28.1 155.4 %all-reduce.3.cloned.1.call-start = ((), (), s32[]{:S(2)}) async-start(), calls=%async_computation.1 | async-start | bytes 2097152 | tf_op jit(solution)/shard_map/psum | solution.py:135
  43.0 0.6 copy-start.6
  63.6 0.6 copy-start.5
  142.9 6.0 %copy-start.10 = (s32[9]{0:T(128)S(1)}, s32[9]{0:T(128)}, u32[]{:S(2)}) copy-start(s32[9]{0:T(128)} %param.29) | copy-start | bytes 112
  143.0 6.7 %copy-start.7 = (f32[768]{0:T(1024)S(1)}, f32[768]{0:T(1024)}, u32[]{:S(2)}) copy-start(f32[768]{0:T(1024)} %multiply_exponential_fusion) | copy-start | bytes 9220
  143.0 43.0 %copy-start.8 = (f32[2048]{0:T(1024)S(1)}, f32[2048]{0:T(1024)}, u32[]{:S(2)}) copy-start(f32[2048]{0:T(1024)} %param.21) | copy-start | bytes 24580
  148.7 75.2 %all-reduce.5.cloned.1.call-start = ((), (), s32[]{:S(2)}) async-start(), calls=%async_computation.2 | async-start | bytes 393216 | tf_op jit(solution)/shard_map/psum | solution.py:141
  185.0 1.0 copy-start.2
  223.9 9.4 %all-to-all-start = ((f32[4,32,384]{2,1,0:T(8,128)}), f32[4,32,384]{2,1,0:T(8,128)}, u32[]{:S(2)}, u32[]{:S(2)}) async-start(f32[4,32,384]{2,1,0:T(8,128)} %all-reduce.5.cloned.1.call-done), calls=%async_computation | async-start | bytes 393216 | tf_op jit(solution)/shard_map/all_to_all | solution.py:144
  240.8 0.7 copy-start.4
  265.2 0.7 copy-start.3
Sparse Core Ops, SparseCore 0:
  28.3 83.8 all-gather.7
  148.8 34.7 all-reduce.2
  188.7 35.1 all-reduce.4
where the time goes:
time: 316 us; the launch traced here: 315 us
  waiting for transfers between devices  101 us (32%)
  blocking collectives  87.2 us (28%)
  other arithmetic  49 us (16%)
  local copies, waits for them, and re-layouts  29.8 us (9%)
  matrix products  28.9 us (9%)
  between operations  14.1 us (4%)
  starting transfers between devices  4.26 us (1%)
    all_gather x3, blocking collectives, prefix_sum(): gathered = lax.all_gather(totals[None], 'tm', axis=0, tiled=True)  46.8 us
    all_gather x1, waiting for transfers between devices, merged(): gathered = jax.tree.map(lambda a: lax.all_gather(a, axis), part)  43.3 us
    psum x1, waiting for transfers between devices, shards(): lax.psum(jnp.dot(attended, out_weight, preferred_element_type=jnp.float32...  33.1 us
    all_gather x2, blocking collectives, merged(): gathered = jax.tree.map(lambda a: lax.all_gather(a, axis), part)  28.1 us
    psum x1, waiting for transfers between devices, shards(): square_sum, cond_sum = lax.psum((squares, cond_part), 'tm')  20.7 us
    dot_general x3, matrix products, shards(): jnp.dot(action.reshape(row_each * time_each, WIDTH), head_out, preferred_...  12.9 us
    psum x1, blocking collectives, shards(): square_sum, cond_sum = lax.psum((squares, cond_part), 'tm')  12.3 us
    add x3, other arithmetic, combine(): out_one * scale_one[:, :, None] + out_two * scale_two[:, :, None]  10.2 us
  transfers between devices with their start and end apart: 4, of which 4 were waited for; matrix products, arithmetic and copies ran while one was open for 5% of the time, Pallas kernels for 0%

commit v1 on v0

v1 whole, which is shorter than its diff:
```python
import functools
import math

import jax
import jax.numpy as jnp
from jax import lax
from jax.experimental import pallas as pl
from jax.experimental.pallas import tpu as pltpu
from jax.sharding import PartitionSpec as P

HD = 128
SWEEPS = 3
LANES = 128
F32 = jnp.float32
BF16 = jnp.bfloat16
VMEM = pl.BlockSpec(memory_space=pltpu.VMEM)
LIMIT = 56 * 1024 * 1024


def greet(axes):
    barrier = pltpu.get_barrier_semaphore()
    count = 0
    for axis in axes:
        n = lax.axis_size(axis)
        me = lax.axis_index(axis)
        for step in range(1, n):
            pl.semaphore_signal(
                barrier,
                inc=1,
                device_id={axis: lax.rem(me + step, n)},
                device_id_type=pl.DeviceIdType.MESH,
            )
        count += n - 1
    pl.semaphore_wait(barrier, count)


def spread(axis, source, target, send, recv):
    n = lax.axis_size(axis)
    me = lax.axis_index(axis)
    copies = []
    for step in range(1, n):
        partner = lax.rem(me + step, n)
        copy = pltpu.make_async_remote_copy(
            src_ref=source(partner),
            dst_ref=target(me),
            send_sem=send.at[step],
            recv_sem=recv.at[step],
            device_id={axis: partner},
            device_id_type=pl.DeviceIdType.MESH,
        )
        copy.start()
        copies.append(copy)
    return copies


def rows_of(index, size):
    return pl.ds(pl.multiple_of(index * size, size), size)


def attend_kernel(valid_ref, q_ref, cos_ref, sin_ref, k_ref, v_ref, out_ref, stats_ref):
    head = pl.program_id(0)
    q = q_ref[...].astype(F32)
    lane = lax.broadcasted_iota(jnp.int32, q.shape, 1)
    other = jnp.where(lane % 2 == 0, -pltpu.roll(q, HD - 1, 1), pltpu.roll(q, 1, 1))
    rotated = (q * cos_ref[...] + other * sin_ref[...]).astype(BF16)
    scores = lax.dot_general(
        rotated, k_ref[...], (((1,), (1,)), ((), ())), preferred_element_type=F32
    ) * (1.0 / math.sqrt(HD))
    valid = lax.broadcasted_iota(jnp.int32, scores.shape, 1) < valid_ref[0]
    masked = jnp.where(valid, scores, F32(-1e30))
    top = jnp.max(masked, axis=1, keepdims=True)
    weights = jnp.where(valid, jnp.exp(masked - top), F32(0.0))
    total = jnp.sum(weights, axis=1, keepdims=True)
    out_ref[...] = jnp.dot(
        weights.astype(BF16), v_ref[...], preferred_element_type=F32
    ).astype(BF16)

    @pl.when(head == 0)
    def _():
        stats_ref[...] = jnp.zeros_like(stats_ref)

    lanes = lax.broadcasted_iota(jnp.int32, stats_ref.shape, 1)
    stats_ref[...] = jnp.where(
        lanes == head, top, jnp.where(lanes == head + LANES // 2, total, stats_ref[...])
    )


def attend(queries, cosine, sine, keys, values, valid):
    rows, width = queries.shape
    count = keys.shape[0]
    per_head = lambda size: pl.BlockSpec((size, HD), lambda h, _: (0, h))
    fixed = lambda: pl.BlockSpec((rows, LANES), lambda h, _: (0, 0))
    return pl.pallas_call(
        attend_kernel,
        grid_spec=pltpu.PrefetchScalarGridSpec(
            num_scalar_prefetch=1,
            grid=(width // HD,),
            in_specs=[per_head(rows), fixed(), fixed(), per_head(count), per_head(count)],
            out_specs=[per_head(rows), fixed()],
        ),
        out_shape=[
            jax.ShapeDtypeStruct((rows, width), BF16),
            jax.ShapeDtypeStruct((rows, LANES), F32),
        ],
        compiler_params=pltpu.CompilerParams(vmem_limit_bytes=LIMIT),
        cost_estimate=pl.CostEstimate(
            flops=4 * rows * count * width,
            bytes_accessed=4 * count * width,
            transcendentals=rows * count * (width // HD),
        ),
    )(valid, queries, cosine, sine, keys, values)


def merge_kernel(out_ref, stats_ref, att_ref, parts, stats, s1, r1, s2, r2, s3, r3):
    n = lax.axis_size("tm")
    me = lax.axis_index("tm")
    rows, width = out_ref.shape
    each = rows // n
    greet(["tm"])
    copies = spread(
        "tm", lambda p: stats_ref.at[rows_of(p, each)], lambda m: stats.at[m], s1, r1
    )
    copies += spread(
        "tm", lambda p: out_ref.at[rows_of(p, each)], lambda m: parts.at[m], s2, r2
    )
    stats[me] = stats_ref[rows_of(me, each), :]
    parts[me] = out_ref[rows_of(me, each), :]
    for copy in copies:
        copy.wait()
    half = LANES // 2
    tops = [stats[i][:, :half] for i in range(n)]
    top = functools.reduce(jnp.maximum, tops)
    factors = [jnp.exp(t - top) for t in tops]
    denom = sum(stats[i][:, half:] * factors[i] for i in range(n))
    mine = rows_of(me, each)
    for head in range(width // HD):
        cols = slice(head * HD, (head + 1) * HD)
        lane = slice(head, head + 1)
        numer = sum(parts[i, :, cols].astype(F32) * factors[i][:, lane] for i in range(n))
        att_ref[mine, cols] = (numer / denom[:, lane]).astype(BF16)
    for copy in spread(
        "tm", lambda p: att_ref.at[mine], lambda m: att_ref.at[rows_of(m, each)], s3, r3
    ):
        copy.wait()


def sems(*axes):
    return [pltpu.SemaphoreType.DMA((lax.axis_size(a),)) for a in axes for _ in range(2)]


def comm_params(ident):
    return pltpu.CompilerParams(
        collective_id=ident, has_side_effects=True, vmem_limit_bytes=LIMIT
    )


def merge(out, stats):
    n = lax.axis_size("tm")
    rows, width = out.shape
    return pl.pallas_call(
        merge_kernel,
        out_shape=jax.ShapeDtypeStruct((rows, width), BF16),
        in_specs=[VMEM] * 2,
        out_specs=VMEM,
        scratch_shapes=[
            pltpu.VMEM((n, rows // n, width), BF16),
            pltpu.VMEM((n, rows // n, LANES), F32),
        ]
        + sems("tm", "tm", "tm"),
        compiler_params=comm_params(1),
    )(out, stats)


def hidden_kernel(
    part_ref, res_ref, gain_ref, noise_ref, scaled_ref, square_ref, got_ref, parts, s1, r1, s2, r2
):
    n = lax.axis_size("heads")
    me = lax.axis_index("heads")
    when = lax.axis_index("tm")
    each = res_ref.shape[0]
    greet(["heads", "tm"])
    copies = spread(
        "heads", lambda p: part_ref.at[rows_of(p, each)], lambda m: parts.at[m], s1, r1
    )
    others = spread("tm", lambda p: noise_ref.at[p], lambda m: got_ref.at[m], s2, r2)
    parts[me] = part_ref[rows_of(me, each), :]
    got_ref[when] = noise_ref[when]
    for copy in copies:
        copy.wait()
    hidden = res_ref[...].astype(F32) + sum(parts[i].astype(F32) for i in range(n))
    squares = jnp.sum(hidden * hidden, axis=1, keepdims=True)
    square_ref[...] = jnp.broadcast_to(squares, square_ref.shape)
    scaled_ref[...] = (hidden * gain_ref[...]).astype(BF16)
    for copy in others:
        copy.wait()


def hidden_rows(partial, residual, gain, noise):
    n = lax.axis_size("heads")
    each, width = residual.shape
    return pl.pallas_call(
        hidden_kernel,
        out_shape=[
            jax.ShapeDtypeStruct((each, width), BF16),
            jax.ShapeDtypeStruct((each, LANES), F32),
            jax.ShapeDtypeStruct(noise.shape, noise.dtype),
        ],
        in_specs=[VMEM] * 4,
        out_specs=[VMEM] * 3,
        scratch_shapes=[pltpu.VMEM((n, each, width), BF16)] + sems("heads", "tm"),
        compiler_params=comm_params(2),
    )(partial, residual, gain, noise)


def sweep_kernel(
    model_width, cond_ref, square_ref, start_ref, emb_ref, step_ref, noise_ref, in_ref, head_ref,
    out_ref, conds, squares, base, states, low, action, s1, r1, s2, r2, s3, r3,
):
    n = lax.axis_size("tm")
    me = lax.axis_index("tm")
    each, chan = start_ref.shape
    width = emb_ref.shape[1]
    times = emb_ref.shape[0]
    block = times // n * each
    greet(["tm"])
    copies = spread("tm", lambda p: cond_ref.at[p], lambda m: conds.at[m], s1, r1)
    copies += spread("tm", lambda p: square_ref.at[p], lambda m: squares.at[m], s2, r2)
    conds[me] = cond_ref[me]
    squares[me] = square_ref[me]
    start = start_ref[...]
    for j in range(times):
        low[j * each : (j + 1) * each, :] = start
    for copy in copies:
        copy.wait()
    square = sum(squares[i][:, :1] for i in range(n))
    inverse = lax.rsqrt(square / model_width + 1e-06)
    condition = sum(conds[i] for i in range(n)) * inverse
    for j in range(times):
        base[j * each : (j + 1) * each, :] = condition + emb_ref[j : j + 1, :]
    tile = 512 if width % 512 == 0 else width
    tile_out = 384 if chan % 384 == 0 else chan

    def sweep(_, carry):
        flat = low[...].astype(BF16)

        def first(i, c):
            cols = pl.ds(pl.multiple_of(i * tile, LANES), tile)
            preact = jnp.dot(flat, in_ref[:, cols], preferred_element_type=F32) + base[:, cols]
            action[:, cols] = jax.nn.silu(preact).astype(BF16)
            return c

        lax.fori_loop(0, width // tile, first, 0)
        act = action[...]

        def second(i, c):
            cols = pl.ds(pl.multiple_of(i * tile_out, LANES), tile_out)
            drift = jnp.dot(act, head_ref[:, cols], preferred_element_type=F32)
            first_state = start_ref[:, cols]
            running = jnp.zeros_like(first_state)
            for j in range(times):
                rows = slice(j * each, (j + 1) * each)
                low[rows, cols] = first_state + running
                if j + 1 < times:
                    step = step_ref[j : j + 1, :1]
                    running = running + (step * drift[rows, :] + noise_ref[rows, cols])
            return c

        lax.fori_loop(0, chan // tile_out, second, 0)
        return carry

    lax.fori_loop(0, SWEEPS, sweep, 0)
    states[...] = low[...]
    out_ref[me] = states[rows_of(me, block), :]
    for copy in spread(
        "tm", lambda p: states.at[rows_of(p, block)], lambda m: out_ref.at[m], s3, r3
    ):
        copy.wait()


def sweeps(model_width, cond, square, start, embedding, step, noise, in_weight, head_out):
    n = lax.axis_size("tm")
    each, chan = start.shape
    times, width = embedding.shape
    return pl.pallas_call(
        functools.partial(sweep_kernel, model_width),
        out_shape=jax.ShapeDtypeStruct((n, times // n * each, chan), F32),
        in_specs=[VMEM] * 8,
        out_specs=VMEM,
        scratch_shapes=[
            pltpu.VMEM(cond.shape, F32),
            pltpu.VMEM(square.shape, F32),
            pltpu.VMEM((times * each, width), F32),
            pltpu.VMEM((times * each, chan), F32),
            pltpu.VMEM((times * each, chan), F32),
            pltpu.VMEM((times * each, width), BF16),
        ]
        + sems("tm", "tm", "tm"),
        compiler_params=comm_params(3),
    )(cond, square, start, embedding, step, noise, in_weight, head_out)


def time_terms(levels, hidden_width):
    half_width = hidden_width // 2
    frequencies = jnp.exp(-math.log(10000.0) * jnp.arange(half_width, dtype=F32) / half_width)
    angles = levels[:-1, None] * frequencies[None, :]
    embedding = jnp.concatenate([jnp.sin(angles), jnp.cos(angles)], axis=1)
    step_size = (levels[:-1] - levels[1:]) / 1000.0
    return (embedding, step_size, jnp.sqrt(step_size))


def shards(
    queries,
    cache_keys,
    cache_values,
    residual,
    out_weight,
    norm_gain,
    cond_weight,
    in_weight,
    head_out,
    start_state,
    noise_draws,
    positions,
    cache_length,
    plan,
):
    n = lax.axis_size("tm")
    when = lax.axis_index("tm")
    head_index = lax.axis_index("heads")
    model_width = norm_gain.shape[0] * n
    key_count = cache_keys.shape[0]
    row_each, time_each, chan = noise_draws.shape
    each = row_each // n
    times = time_each * n
    width = in_weight.shape[1]

    cond_all = lax.all_gather(cond_weight, "heads")

    pair = jnp.arange(HD, dtype=jnp.int32) // 2
    frequencies = jnp.exp(-math.log(10000.0) * 2.0 * pair.astype(F32) / HD)
    angles = positions.astype(F32)[:, None] * frequencies[None, :]
    valid = cache_length - when.astype(jnp.int32) * key_count
    out, stats = attend(
        queries, jnp.cos(angles), jnp.sin(angles), cache_keys, cache_values, valid
    )
    attended = merge(out, stats)
    partial = jnp.dot(attended, out_weight, preferred_element_type=F32).astype(BF16)

    noise = noise_draws.reshape(n, each, time_each, chan).transpose(0, 2, 1, 3)
    noise = noise.reshape(n, time_each * each, chan)
    own_rows = lax.dynamic_slice_in_dim(residual, head_index * row_each, row_each, 0)
    scaled, square, noise = hidden_rows(partial, own_rows, norm_gain[None, :], noise)

    cond = jnp.einsum("rk,hkc->rhc", scaled, cond_all, preferred_element_type=F32)
    cond = cond.reshape(n, each, width)
    embedding, step_size, noise_scale = time_terms(plan.astype(F32), width)
    noise_term = noise.astype(F32).reshape(times, each, chan) * noise_scale[:, None, None]
    start = lax.dynamic_slice_in_dim(start_state, when * each, each, 0)
    states = sweeps(
        model_width,
        cond,
        square.reshape(n, each, LANES),
        start,
        embedding,
        jnp.broadcast_to(step_size[:, None], (times, LANES)),
        noise_term.reshape(times * each, chan),
        in_weight,
        head_out,
    )
    states = states.reshape(n, time_each, each, chan).transpose(0, 2, 1, 3)
    return states.reshape(row_each, time_each, chan)


def solution(mesh):
    placed = (
        P("groups", "heads"),
        P(("groups", "tm"), "heads"),
        P(("groups", "tm"), "heads"),
        P("groups", "tm"),
        P("heads", "tm"),
        P("tm"),
        P("tm", "heads"),
        P(),
        P(),
        P(("groups", "heads"), None),
        P(("groups", "heads"), "tm", None),
        P("groups"),
        P("groups"),
        P(),
    )
    return jax.shard_map(
        shards,
        mesh=mesh,
        in_specs=placed,
        out_specs=P(("groups", "heads"), "tm", None),
        check_vma=False,
    )
```

time: 316 us -> 123 us (0.39)
  waiting for transfers between devices: 101 us -> 0.71 us
  blocking collectives: 87.2 us -> 0 us
  Pallas kernels: 0 us -> 85.9 us
  other arithmetic: 49 us -> 4.89 us
  local copies, waits for them, and re-layouts: 29.8 us -> 7.19 us
  matrix products: 28.9 us -> 9.63 us
  starting transfers between devices: 4.26 us -> 0.01 us
    pallas_call x0 -> x4, Pallas kernels: none -> 85.9 us  [the longest x1 31.1 us: merge(): pl.pallas_call(merge_kernel, out_shape=jax.ShapeDtypeStruct((rows, width)...]
    all_gather x5 -> x0, blocking collectives: 74.9 us -> none  [the longest x3 46.8 us: prefix_sum(): gathered = lax.all_gather(totals[None], 'tm', axis=0, tiled=True)]
    psum x2 -> x0, waiting for transfers between devices: 53.8 us -> none  [the longest x1 33.1 us: shards(): lax.psum(jnp.dot(attended, out_weight, preferred_element_type=jnp.float32...]
    all_gather x1, waiting for transfers between devices: 43.3 us -> 0.01 us  [shards(): cond_all = lax.all_gather(cond_weight, 'heads')]
    add x11 -> x0, other arithmetic: 20.8 us -> none  [the longest x3 10.2 us: combine(): out_one * scale_one[:, :, None] + out_two * scale_two[:, :, None]]
    dot_general x7 -> x2, matrix products: 28.9 us -> 9.63 us  [the longest x1 5.64 us: shards(): jnp.dot(attended, out_weight, preferred_element_type=F32).astype(BF16)]
    psum x1 -> x0, blocking collectives: 12.3 us -> none  [shards(): square_sum, cond_sum = lax.psum((squares, cond_part), 'tm')]
    unnamed x23 -> x2, local copies, waits for them, and re-layouts: 8.93 us -> 0.01 us
  transfers between devices with their start and end apart: 4 -> 1, of which waited for: 4 -> 0; matrix products, arithmetic and copies ran while one was open for 5% -> 12% of each run, Pallas kernels for 0% -> 48%
where the time goes in v1:
time: 123 us; the launch traced here: 122 us
  Pallas kernels  85.9 us (70%)
  between operations  14.1 us (11%)
  matrix products  9.63 us (8%)
  local copies, waits for them, and re-layouts  7.19 us (6%)
  other arithmetic  4.89 us (4%)
    pallas_call x1, Pallas kernels, merge(): pl.pallas_call(merge_kernel, out_shape=jax.ShapeDtypeStruct((rows, width)...  31.1 us
    pallas_call x1, Pallas kernels, sweeps(): pl.pallas_call(functools.partial(sweep_kernel, model_width), out_shape=ja...  26.6 us
    pallas_call x1, Pallas kernels, attend(): pl.pallas_call(attend_kernel, grid_spec=pltpu.PrefetchScalarGridSpec(num_...  15.2 us
    pallas_call x1, Pallas kernels, hidden_rows(): pl.pallas_call(hidden_kernel, out_shape=[jax.ShapeDtypeStruct((each, widt...  13 us
    dot_general x1, matrix products, shards(): jnp.dot(attended, out_weight, preferred_element_type=F32).astype(BF16)  5.64 us
    dot_general x1, matrix products, shards(): jnp.einsum('rk,hkc->rhc', scaled, cond_all, preferred_element_type=F32)  3.99 us
  transfers between devices with their start and end apart: 1, of which 0 were waited for; matrix products, arithmetic and copies ran while one was open for 12% of the time, Pallas kernels for 48%

profile of v1, /device:TPU:0, one launch (start us, length us, event | category | flops | bytes accessed | tf_op | source)
XLA Modules:
  0.0 122.4 jit_solution(5904873890001274014)
XLA Ops:
  6.5 0.0 copy-start
  6.5 0.0 all-gather.3.cloned.1.call-start
  6.5 0.7 all-gather.3.cloned.1.call-update
  7.9 0.7 convert_element_type.17
  8.6 1.6 %copy.19 = bf16[4,8,2,1152]{3,1,2,0:T(8,128)(2,1)} copy(bf16[4,8,2,1152]{3,2,1,0:T(2,128)(2,1)} %bitcast.26) | data formatting | bytes 294912 | tf_op jit(solution)/shard_map/reshape | solution.py:349
  10.2 0.7 convert_element_type.20
  10.8 0.1 fusion.5
  10.9 0.1 mul.63
  11.0 0.1 mul.64
  11.1 1.0 multiply_sine_fusion
  12.0 15.2 %shard_map.136 = (bf16[128,2048]{1,0:T(8,128)(2,1)}, f32[128,128]{1,0:T(8,128)}) custom-call(s32[1]{0:T(128)S(6)} %sub.16.valid_ref, bf16[128,2048]{1,0:T(8,128)(2,1)} %q_ref.1, f32[128,128]{1,0:T(8,128)} %get-tuple-element.20.cos_ref, f32[128,128]{1,0:T(8,128)} %get-tuple-element.19.sin_ref, bf16[1024,2048]{1,0:T(8,128)(2,1)} %k_ref.1, bf16[1024,2048]{1,0:T(8,128)(2,1)} %v_ref.1), custom_call_target="tpu_custom_call" | custom-call | flops 1073741824 | bytes 8388608 | tf_op jit(solution)/shard_map/pallas_call | solution.py:93
  27.3 31.1 %shard_map.137 = bf16[128,2048]{1,0:T(8,128)(2,1)} custom-call(bf16[128,2048]{1,0:T(8,128)(2,1)} %get-tuple-element.10.out_ref, f32[128,128]{1,0:T(8,128)} %get-tuple-element.11.stats_ref), custom_call_target="tpu_custom_call" | custom-call | tf_op jit(solution)/shard_map/pallas_call | solution.py:160
  58.3 0.0 copy-done
  58.3 0.7 constant_dynamic-slice_fusion.1.res_ref
  59.0 5.6 %convolution_convert_fusion.part_ref = bf16[128,2048]{1,0:T(8,128)(2,1)} fusion(bf16[128,2048]{1,0:T(8,128)(2,1)} %shard_map.137, bf16[2048,2048]{1,0:T(8,128)(2,1)} %param.18), kind=kOutput, calls=%fused_computation | convolution fusion | flops 1074003968 | bytes 9437184 | tf_op jit(solution)/shard_map/dot_general | solution.py:347
  64.7 13.0 %shard_map.138 = (bf16[32,2048]{1,0:T(8,128)(2,1)}, f32[32,128]{1,0:T(8,128)}, bf16[4,16,1152]{2,1,0:T(8,128)(2,1)}) custom-call(bf16[128,2048]{1,0:T(8,128)(2,1)} %convolution_convert_fusion.part_ref, bf16[32,2048]{1,0:T(8,128)(2,1)} %constant_dynamic-slice_fusion.1.res_ref, f32[1,2048]{1,0:T(1,128)} %bitcast.28, bf16[4,16,1152]{2,1,0:T(8,128)(2,1)} %bitcast.25), custom_call_target="tpu_custom_call" | custom-call | tf_op jit(solution)/shard_map/pallas_call | solution.py:201
  77.7 0.2 multiply_sine_fusion.1
  77.8 1.4 %constant_dynamic-slice_fusion.start_ref = f32[8,1152]{1,0:T(8,128)} fusion(f32[32,1152]{1,0:T(8,128)} %param.23, s32[]{:T(128)S(6)} %select_n.17), kind=kLoop, calls=%fused_computation.19 | loop fusion | bytes 73732 | tf_op jit(solution)/shard_map/dynamic_slice | solution.py:358
  79.2 0.6 pad_maximum_fusion.emb_ref
  79.9 1.7 %convert_multiply_fusion.noise_ref = f32[64,1152]{1,0:T(8,128)} fusion(bf16[4,16,1152]{2,1,0:T(8,128)(2,1)} %get-tuple-element.14, f32[64]{0:T(128)S(1)} %mul.64), kind=kLoop, calls=%fused_computation.1 | loop fusion | flops 147456 | bytes 442624 | tf_op jit(solution)/shard_map/mul | solution.py:357
  81.6 0.0 all-gather.3.cloned.1.call-done
  81.6 4.0 %fusion = f32[32,4,384]{2,0,1:T(8,128)S(1)} fusion(bf16[4,2048,384]{2,1,0:T(8,128)(2,1)} %bitcast.23, bf16[32,2048]{1,0:T(8,128)(2,1)} %get-tuple-element.12), kind=kOutput, calls=%fused_computation.3 | convolution fusion | flops 201326592 | bytes 6619136 | tf_op jit(solution)/shard_map/rk,hkc->rhc/dot_general | solution.py:354
  85.6 0.1 copy.16
  85.7 0.8 reshape.54.cond_ref
  86.5 0.7 broadcast_in_dim.5.step_ref
  87.1 26.6 %shard_map.139 = f32[4,16,1152]{2,1,0:T(8,128)} custom-call(f32[4,8,1536]{2,1,0:T(8,128)} %reshape.54.cond_ref, f32[4,8,128]{2,1,0:T(8,128)} %bitcast.27, f32[8,1152]{1,0:T(8,128)} %constant_dynamic-slice_fusion.start_ref, f32[8,1536]{1,0:T(8,128)} %pad_maximum_fusion.emb_ref, f32[8,128]{1,0:T(8,128)} %broadcast_in_dim.5.step_ref, ...), custom_call_target="tpu_custom_call" | custom-call | tf_op jit(solution)/shard_map/pallas_call | solution.py:284
  113.8 1.8 %copy.17 = f32[4,8,2,1152]{3,2,1,0:T(2,128)} copy(f32[4,8,2,1152]{3,1,2,0:T(8,128)} %bitcast.24) | data formatting | bytes 589824 | tf_op jit(solution)/shard_map/transpose | solution.py:370
  (2 shorter events, 0.0 us)
Async XLA Ops:
  6.5 51.8 %copy-start = (bf16[128,2048]{1,0:T(8,128)(2,1)S(1)}, bf16[128,2048]{1,0:T(8,128)(2,1)}, u32[]{:S(2)}) copy-start(bf16[128,2048]{1,0:T(8,128)(2,1)} %param.17) | copy-start | bytes 1572868
  6.5 75.0 %all-gather.3.cloned.1.call-start = ((), (), s32[]{:S(2)}) async-start(), calls=%async_computation | async-start | bytes 7864320 | tf_op jit(solution)/shard_map/all_gather | solution.py:337
Sparse Core Ops, SparseCore 0:
  8.9 49.0 all-gather.2

commit v2 on v1

--- a/solution.py
+++ b/solution.py
@@ -11,6 +11,7 @@
 HD = 128
 SWEEPS = 3
 LANES = 128
+HEADS_AT_ONCE = 8
 F32 = jnp.float32
 BF16 = jnp.bfloat16
 VMEM = pl.BlockSpec(memory_space=pltpu.VMEM)
@@ -48,127 +49,150 @@
             device_id={axis: partner},
             device_id_type=pl.DeviceIdType.MESH,
         )
-        copy.start()
         copies.append(copy)
     return copies
 
 
+def launch(copies):
+    for copy in copies:
+        copy.start()
+    return copies
+
+
 def rows_of(index, size):
     return pl.ds(pl.multiple_of(index * size, size), size)
 
 
-def attend_kernel(valid_ref, q_ref, cos_ref, sin_ref, k_ref, v_ref, out_ref, stats_ref):
-    head = pl.program_id(0)
-    q = q_ref[...].astype(F32)
-    lane = lax.broadcasted_iota(jnp.int32, q.shape, 1)
-    other = jnp.where(lane % 2 == 0, -pltpu.roll(q, HD - 1, 1), pltpu.roll(q, 1, 1))
-    rotated = (q * cos_ref[...] + other * sin_ref[...]).astype(BF16)
-    scores = lax.dot_general(
-        rotated, k_ref[...], (((1,), (1,)), ((), ())), preferred_element_type=F32
-    ) * (1.0 / math.sqrt(HD))
-    valid = lax.broadcasted_iota(jnp.int32, scores.shape, 1) < valid_ref[0]
-    masked = jnp.where(valid, scores, F32(-1e30))
-    top = jnp.max(masked, axis=1, keepdims=True)
-    weights = jnp.where(valid, jnp.exp(masked - top), F32(0.0))
-    total = jnp.sum(weights, axis=1, keepdims=True)
-    out_ref[...] = jnp.dot(
-        weights.astype(BF16), v_ref[...], preferred_element_type=F32
-    ).astype(BF16)
-
-    @pl.when(head == 0)
+def attend_kernel(
+    valid_ref, q_ref, cos_ref, sin_ref, k_ref, v_ref, out_ref,
+    outs, sides, parts, stats, merged, s1, r1, s2, r2, s3, r3,
+):
+    group = pl.program_id(0)
+    groups, rows, width = outs.shape
+    n = lax.axis_size("tm")
+    me = lax.axis_index("tm")
+    each = rows // n
+    half = LANES // 2
+    mine = rows_of(me, each)
+
+    def scatter(g):
+        return spread(
+            "tm", lambda p: sides.at[g, rows_of(p, each)], lambda m: stats.at[g, m],
+            s1.at[g], r1.at[g],
+        ) + spread(
+            "tm", lambda p: outs.at[g, rows_of(p, each)], lambda m: parts.at[g, m],
+            s2.at[g], r2.at[g],
+        )
+
+    def gather(g):
+        return spread(
+            "tm", lambda p: merged.at[g, mine], lambda m: merged.at[g, rows_of(m, each)],
+            s3.at[g], r3.at[g],
+        )
+
+    def finish(copies):
+        for copy in copies:
+            copy.wait()
+
+    def combine(g):
+        finish(scatter(g))
+        tops = [stats[g, i, :, :half] for i in range(n)]
+        top = functools.reduce(jnp.maximum, tops)
+        factors = [jnp.exp(t - top) for t in tops]
+        denom = sum(stats[g, i, :, half:] * factors[i] for i in range(n))
+        for head in range(width // HD):
+            cols = slice(head * HD, (head + 1) * HD)
+            lane = slice(head, head + 1)
+            numer = sum(
+                parts[g, i, :, cols].astype(F32) * factors[i][:, lane] for i in range(n)
+            )
+            merged[g, mine, cols] = (numer / denom[:, lane]).astype(BF16)
+        launch(gather(g))
+
+    @pl.when(group == 0)
     def _():
-        stats_ref[...] = jnp.zeros_like(stats_ref)
-
-    lanes = lax.broadcasted_iota(jnp.int32, stats_ref.shape, 1)
-    stats_ref[...] = jnp.where(
-        lanes == head, top, jnp.where(lanes == head + LANES // 2, total, stats_ref[...])
+        greet(["tm"])
+
+    lane = lax.broadcasted_iota(jnp.int32, (rows, HD), 1)
+    even = lane % 2 == 0
+    valid = lax.broadcasted_iota(jnp.int32, (rows, k_ref.shape[0]), 1) < valid_ref[0]
+    side = jnp.zeros((rows, LANES), F32)
+    for head in range(width // HD):
+        cols = slice(head * HD, (head + 1) * HD)
+        q = q_ref[:, cols].astype(F32)
+        other = jnp.where(even, -pltpu.roll(q, HD - 1, 1), pltpu.roll(q, 1, 1))
+        rotated = (q * cos_ref[...] + other * sin_ref[...]).astype(BF16)
+        scores = lax.dot_general(
+            rotated, k_ref[:, cols], (((1,), (1,)), ((), ())), preferred_element_type=F32
+        ) * (1.0 / math.sqrt(HD))
+        masked = jnp.where(valid, scores, F32(-1e30))
+        top = jnp.max(masked, axis=1, keepdims=True)
+        weights = jnp.where(valid, jnp.exp(masked - top), F32(0.0))
+        total = jnp.sum(weights, axis=1, keepdims=True)
+        outs[group, :, cols] = jnp.dot(
+            weights.astype(BF16), v_ref[:, cols], preferred_element_type=F32
+        ).astype(BF16)
+        side = jnp.where(lane == head, top, jnp.where(lane == head + half, total, side))
+    sides[group] = side
+    launch(scatter(group))
+    stats[group, me] = sides[group, mine, :]
+    parts[group, me] = outs[group, mine, :]
+
+    @pl.when(group > 0)
+    def _():
+        combine(group - 1)
+
+    @pl.when(group == groups - 1)
+    def _():
+        combine(group)
+        for g in range(groups):
+            finish(gather(g))
+            out_ref[:, g * width : (g + 1) * width] = merged[g]
+
+
+def sems(*axes):
+    return [pltpu.SemaphoreType.DMA((lax.axis_size(a),)) for a in axes for _ in range(2)]
+
+
+def comm_params(ident):
+    return pltpu.CompilerParams(
+        collective_id=ident, has_side_effects=True, vmem_limit_bytes=LIMIT
     )
 
 
 def attend(queries, cosine, sine, keys, values, valid):
     rows, width = queries.shape
     count = keys.shape[0]
-    per_head = lambda size: pl.BlockSpec((size, HD), lambda h, _: (0, h))
-    fixed = lambda: pl.BlockSpec((rows, LANES), lambda h, _: (0, 0))
+    n = lax.axis_size("tm")
+    part = HD * math.gcd(width // HD, HEADS_AT_ONCE)
+    groups = width // part
+    cut = lambda size: pl.BlockSpec((size, part), lambda g: (0, g))
+    fixed = lambda size: pl.BlockSpec((rows, size), lambda g: (0, 0))
+    sem = pltpu.SemaphoreType.DMA((groups, n))
     return pl.pallas_call(
         attend_kernel,
-        grid_spec=pltpu.PrefetchScalarGridSpec(
-            num_scalar_prefetch=1,
-            grid=(width // HD,),
-            in_specs=[per_head(rows), fixed(), fixed(), per_head(count), per_head(count)],
-            out_specs=[per_head(rows), fixed()],
-        ),
-        out_shape=[
-            jax.ShapeDtypeStruct((rows, width), BF16),
-            jax.ShapeDtypeStruct((rows, LANES), F32),
+        grid=(groups,),
+        in_specs=[
+            pl.BlockSpec(memory_space=pltpu.SMEM),
+            cut(rows), fixed(LANES), fixed(LANES), cut(count), cut(count),
         ],
-        compiler_params=pltpu.CompilerParams(vmem_limit_bytes=LIMIT),
+        out_specs=fixed(width),
+        out_shape=jax.ShapeDtypeStruct((rows, width), BF16),
+        scratch_shapes=[
+            pltpu.VMEM((groups, rows, part), BF16),
+            pltpu.VMEM((groups, rows, LANES), F32),
+            pltpu.VMEM((groups, n, rows // n, part), BF16),
+            pltpu.VMEM((groups, n, rows // n, LANES), F32),
+            pltpu.VMEM((groups, rows, part), BF16),
+        ]
+        + [sem] * 6,
+        compiler_params=comm_params(1),
         cost_estimate=pl.CostEstimate(
             flops=4 * rows * count * width,
             bytes_accessed=4 * count * width,
             transcendentals=rows * count * (width // HD),
         ),
     )(valid, queries, cosine, sine, keys, values)
-
-
-def merge_kernel(out_ref, stats_ref, att_ref, parts, stats, s1, r1, s2, r2, s3, r3):
-    n = lax.axis_size("tm")
-    me = lax.axis_index("tm")
-    rows, width = out_ref.shape
-    each = rows // n
-    greet(["tm"])
-    copies = spread(
-        "tm", lambda p: stats_ref.at[rows_of(p, each)], lambda m: stats.at[m], s1, r1
-    )
-    copies += spread(
-        "tm", lambda p: out_ref.at[rows_of(p, each)], lambda m: parts.at[m], s2, r2
-    )
-    stats[me] = stats_ref[rows_of(me, each), :]
-    parts[me] = out_ref[rows_of(me, each), :]
-    for copy in copies:
-        copy.wait()
-    half = LANES // 2
-    tops = [stats[i][:, :half] for i in range(n)]
-    top = functools.reduce(jnp.maximum, tops)
-    factors = [jnp.exp(t - top) for t in tops]
-    denom = sum(stats[i][:, half:] * factors[i] for i in range(n))
-    mine = rows_of(me, each)
-    for head in range(width // HD):
-        cols = slice(head * HD, (head + 1) * HD)
-        lane = slice(head, head + 1)
-        numer = sum(parts[i, :, cols].astype(F32) * factors[i][:, lane] for i in range(n))
-        att_ref[mine, cols] = (numer / denom[:, lane]).astype(BF16)
-    for copy in spread(
-        "tm", lambda p: att_ref.at[mine], lambda m: att_ref.at[rows_of(m, each)], s3, r3
-    ):
-        copy.wait()
-
-
-def sems(*axes):
-    return [pltpu.SemaphoreType.DMA((lax.axis_size(a),)) for a in axes for _ in range(2)]
-
-
-def comm_params(ident):
-    return pltpu.CompilerParams(
-        collective_id=ident, has_side_effects=True, vmem_limit_bytes=LIMIT
-    )
-
-
-def merge(out, stats):
-    n = lax.axis_size("tm")
-    rows, width = out.shape
-    return pl.pallas_call(
-        merge_kernel,
-        out_shape=jax.ShapeDtypeStruct((rows, width), BF16),
-        in_specs=[VMEM] * 2,
-        out_specs=VMEM,
-        scratch_shapes=[
-            pltpu.VMEM((n, rows // n, width), BF16),
-            pltpu.VMEM((n, rows // n, LANES), F32),
-        ]
-        + sems("tm", "tm", "tm"),
-        compiler_params=comm_params(1),
-    )(out, stats)
 
 
 def hidden_kernel(
@@ -179,10 +203,12 @@
     when = lax.axis_index("tm")
     each = res_ref.shape[0]
     greet(["heads", "tm"])
-    copies = spread(
-        "heads", lambda p: part_ref.at[rows_of(p, each)], lambda m: parts.at[m], s1, r1
-    )
-    others = spread("tm", lambda p: noise_ref.at[p], lambda m: got_ref.at[m], s2, r2)
+    copies = launch(
+        spread("heads", lambda p: part_ref.at[rows_of(p, each)], lambda m: parts.at[m], s1, r1)
+    )
+    others = launch(
+        spread("tm", lambda p: noise_ref.at[p], lambda m: got_ref.at[m], s2, r2)
+    )
     parts[me] = part_ref[rows_of(me, each), :]
     got_ref[when] = noise_ref[when]
     for copy in copies:
@@ -223,8 +249,10 @@
     times = emb_ref.shape[0]
     block = times // n * each
     greet(["tm"])
-    copies = spread("tm", lambda p: cond_ref.at[p], lambda m: conds.at[m], s1, r1)
-    copies += spread("tm", lambda p: square_ref.at[p], lambda m: squares.at[m], s2, r2)
+    copies = launch(spread("tm", lambda p: cond_ref.at[p], lambda m: conds.at[m], s1, r1))
+    copies += launch(
+        spread("tm", lambda p: square_ref.at[p], lambda m: squares.at[m], s2, r2)
+    )
     conds[me] = cond_ref[me]
     squares[me] = square_ref[me]
     start = start_ref[...]
@@ -271,8 +299,8 @@
     lax.fori_loop(0, SWEEPS, sweep, 0)
     states[...] = low[...]
     out_ref[me] = states[rows_of(me, block), :]
-    for copy in spread(
-        "tm", lambda p: states.at[rows_of(p, block)], lambda m: out_ref.at[m], s3, r3
+    for copy in launch(
+        spread("tm", lambda p: states.at[rows_of(p, block)], lambda m: out_ref.at[m], s3, r3)
     ):
         copy.wait()
 
@@ -340,10 +368,9 @@
     frequencies = jnp.exp(-math.log(10000.0) * 2.0 * pair.astype(F32) / HD)
     angles = positions.astype(F32)[:, None] * frequencies[None, :]
     valid = cache_length - when.astype(jnp.int32) * key_count
-    out, stats = attend(
+    attended = attend(
         queries, jnp.cos(angles), jnp.sin(angles), cache_keys, cache_values, valid
     )
-    attended = merge(out, stats)
     partial = jnp.dot(attended, out_weight, preferred_element_type=F32).astype(BF16)
 
     noise = noise_draws.reshape(n, each, time_each, chan).transpose(0, 2, 1, 3)

time: 123 us -> 112 us (0.911)
  Pallas kernels: 85.9 us -> 75.3 us
    pallas_call x2 -> x1, Pallas kernels: 46.3 us -> 39.1 us  [attend(): pl.pallas_call(attend_kernel, grid=(groups,), in_specs=[pl.BlockSpec(memo...]
    pallas_call x1, Pallas kernels: 13 us -> 9.8 us  [hidden_rows(): pl.pallas_call(hidden_kernel, out_shape=[jax.ShapeDtypeStruct((each, widt...]
  transfers between devices with their start and end apart: 1 -> 1, of which waited for: 0 -> 0; matrix products, arithmetic and copies ran while one was open for 12% -> 13% of each run, Pallas kernels for 48% -> 44%
where the time goes in v2:
time: 112 us
  Pallas kernels  75.3 us (67%)
  between operations  14.1 us (13%)
  matrix products  9.71 us (9%)
  local copies, waits for them, and re-layouts  7.17 us (6%)
  other arithmetic  4.88 us (4%)
    pallas_call x1, Pallas kernels, attend(): pl.pallas_call(attend_kernel, grid=(groups,), in_specs=[pl.BlockSpec(memo...  39.1 us
    pallas_call x1, Pallas kernels, sweeps(): pl.pallas_call(functools.partial(sweep_kernel, model_width), out_shape=ja...  26.4 us
    pallas_call x1, Pallas kernels, hidden_rows(): pl.pallas_call(hidden_kernel, out_shape=[jax.ShapeDtypeStruct((each, widt...  9.8 us
    dot_general x1, matrix products, shards(): jnp.dot(attended, out_weight, preferred_element_type=F32).astype(BF16)  5.71 us
    dot_general x1, matrix products, shards(): jnp.einsum('rk,hkc->rhc', scaled, cond_all, preferred_element_type=F32)  4 us
  transfers between devices with their start and end apart: 1, of which 0 were waited for; matrix products, arithmetic and copies ran while one was open for 13% of the time, Pallas kernels for 44%

profile of v2, /device:TPU:0, one launch (start us, length us, event | category | flops | bytes accessed | tf_op | source)
XLA Modules:
  0.0 111.8 jit_solution(11264561299832213736)
XLA Ops:
  6.5 0.0 copy-start
  6.5 0.0 all-gather.3.cloned.1.call-start
  6.5 0.7 all-gather.3.cloned.1.call-update
  7.9 0.7 convert_element_type.17
  8.6 1.6 %copy.19 = bf16[4,8,2,1152]{3,1,2,0:T(8,128)(2,1)} copy(bf16[4,8,2,1152]{3,2,1,0:T(2,128)(2,1)} %bitcast.26) | data formatting | bytes 294912 | tf_op jit(solution)/shard_map/reshape | solution.py:376
  10.2 0.7 convert_element_type.20
  10.8 0.1 fusion.5
  10.9 0.1 mul.63
  11.0 0.1 mul.64
  11.1 1.0 multiply_sine_fusion
  12.0 39.1 %shard_map.136 = bf16[128,2048]{1,0:T(8,128)(2,1)} custom-call(s32[1]{0:T(128)S(6)} %sub.16.valid_ref, bf16[128,2048]{1,0:T(8,128)(2,1)} %q_ref.1, f32[128,128]{1,0:T(8,128)} %get-tuple-element.16.cos_ref, f32[128,128]{1,0:T(8,128)} %get-tuple-element.15.sin_ref, bf16[1024,2048]{1,0:T(8,128)(2,1)} %k_ref.1, bf16[1024,2048]{1,0:T(8,128)(2,1)} %v_ref.1), custom_call_target="tpu_custom_call" | custom-call | flops 1073741824 | bytes 8388608 | tf_op jit(solution)/shard_map/pallas_call | solution.py:172
  51.1 0.0 copy-done
  51.1 0.7 constant_dynamic-slice_fusion.1.res_ref
  51.8 5.7 %convolution_convert_fusion.part_ref = bf16[128,2048]{1,0:T(8,128)(2,1)} fusion(bf16[128,2048]{1,0:T(8,128)(2,1)} %shard_map.136, bf16[2048,2048]{1,0:T(8,128)(2,1)} %param.18), kind=kOutput, calls=%fused_computation | convolution fusion | flops 1074003968 | bytes 9437184 | tf_op jit(solution)/shard_map/dot_general | solution.py:374
  57.5 9.8 %shard_map.137 = (bf16[32,2048]{1,0:T(8,128)(2,1)}, f32[32,128]{1,0:T(8,128)}, bf16[4,16,1152]{2,1,0:T(8,128)(2,1)}) custom-call(bf16[128,2048]{1,0:T(8,128)(2,1)} %convolution_convert_fusion.part_ref, bf16[32,2048]{1,0:T(8,128)(2,1)} %constant_dynamic-slice_fusion.1.res_ref, f32[1,2048]{1,0:T(1,128)} %bitcast.28, bf16[4,16,1152]{2,1,0:T(8,128)(2,1)} %bitcast.25), custom_call_target="tpu_custom_call" | custom-call | tf_op jit(solution)/shard_map/pallas_call | solution.py:227
  67.3 0.2 multiply_sine_fusion.1
  67.5 1.4 %constant_dynamic-slice_fusion.start_ref = f32[8,1152]{1,0:T(8,128)} fusion(f32[32,1152]{1,0:T(8,128)} %param.23, s32[]{:T(128)S(6)} %select_n.17), kind=kLoop, calls=%fused_computation.19 | loop fusion | bytes 73732 | tf_op jit(solution)/shard_map/dynamic_slice | solution.py:385
  68.9 0.6 pad_maximum_fusion.emb_ref
  69.5 1.7 %convert_multiply_fusion.noise_ref = f32[64,1152]{1,0:T(8,128)} fusion(bf16[4,16,1152]{2,1,0:T(8,128)(2,1)} %get-tuple-element.10, f32[64]{0:T(128)S(1)} %mul.64), kind=kLoop, calls=%fused_computation.1 | loop fusion | flops 147456 | bytes 442624 | tf_op jit(solution)/shard_map/mul | solution.py:384
  71.2 0.0 all-gather.3.cloned.1.call-done
  71.2 4.0 %fusion = f32[32,4,384]{2,0,1:T(8,128)S(1)} fusion(bf16[4,2048,384]{2,1,0:T(8,128)(2,1)} %bitcast.23, bf16[32,2048]{1,0:T(8,128)(2,1)} %get-tuple-element.8), kind=kOutput, calls=%fused_computation.3 | convolution fusion | flops 201326592 | bytes 6619136 | tf_op jit(solution)/shard_map/rk,hkc->rhc/dot_general | solution.py:381
  75.2 0.1 copy.16
  75.3 0.8 reshape.54.cond_ref
  76.1 0.7 broadcast_in_dim.5.step_ref
  76.8 26.4 %shard_map.138 = f32[4,16,1152]{2,1,0:T(8,128)} custom-call(f32[4,8,1536]{2,1,0:T(8,128)} %reshape.54.cond_ref, f32[4,8,128]{2,1,0:T(8,128)} %bitcast.27, f32[8,1152]{1,0:T(8,128)} %constant_dynamic-slice_fusion.start_ref, f32[8,1536]{1,0:T(8,128)} %pad_maximum_fusion.emb_ref, f32[8,128]{1,0:T(8,128)} %broadcast_in_dim.5.step_ref, ...), custom_call_target="tpu_custom_call" | custom-call | tf_op jit(solution)/shard_map/pallas_call | solution.py:312
  103.2 1.8 %copy.17 = f32[4,8,2,1152]{3,2,1,0:T(2,128)} copy(f32[4,8,2,1152]{3,1,2,0:T(8,128)} %bitcast.24) | data formatting | bytes 589824 | tf_op jit(solution)/shard_map/transpose | solution.py:397
  (2 shorter events, 0.0 us)
Async XLA Ops:
  6.5 44.6 %copy-start = (bf16[128,2048]{1,0:T(8,128)(2,1)S(1)}, bf16[128,2048]{1,0:T(8,128)(2,1)}, u32[]{:S(2)}) copy-start(bf16[128,2048]{1,0:T(8,128)(2,1)} %param.17) | copy-start | bytes 1572868
  6.5 64.7 %all-gather.3.cloned.1.call-start = ((), (), s32[]{:S(2)}) async-start(), calls=%async_computation | async-start | bytes 7864320 | tf_op jit(solution)/shard_map/all_gather | solution.py:365
Sparse Core Ops, SparseCore 0:
  8.9 49.0 all-gather.2

commit v3 on v2

--- a/solution.py
+++ b/solution.py
@@ -11,7 +11,7 @@
 HD = 128
 SWEEPS = 3
 LANES = 128
-HEADS_AT_ONCE = 8
+HEADS_AT_ONCE = 4
 F32 = jnp.float32
 BF16 = jnp.bfloat16
 VMEM = pl.BlockSpec(memory_space=pltpu.VMEM)
@@ -65,19 +65,19 @@
 
 def attend_kernel(
     valid_ref, q_ref, cos_ref, sin_ref, k_ref, v_ref, out_ref,
-    outs, sides, parts, stats, merged, s1, r1, s2, r2, s3, r3,
+    outs, sides, parts, stats, turned, merged, s1, r1, s2, r2, s3, r3,
 ):
     group = pl.program_id(0)
     groups, rows, width = outs.shape
     n = lax.axis_size("tm")
     me = lax.axis_index("tm")
     each = rows // n
-    half = LANES // 2
+    count = width // HD
     mine = rows_of(me, each)
 
     def scatter(g):
         return spread(
-            "tm", lambda p: sides.at[g, rows_of(p, each)], lambda m: stats.at[g, m],
+            "tm", lambda p: sides.at[g], lambda m: stats.at[g, m],
             s1.at[g], r1.at[g],
         ) + spread(
             "tm", lambda p: outs.at[g, rows_of(p, each)], lambda m: parts.at[g, m],
@@ -96,10 +96,13 @@
 
     def combine(g):
         finish(scatter(g))
-        tops = [stats[g, i, :, :half] for i in range(n)]
+        rest = jnp.zeros((LANES - stats.shape[2], rows), F32)
+        for i in range(n):
+            turned[i] = jnp.concatenate([stats[g, i], rest], axis=0).T
+        tops = [turned[i, mine, :] for i in range(n)]
         top = functools.reduce(jnp.maximum, tops)
         factors = [jnp.exp(t - top) for t in tops]
-        denom = sum(stats[g, i, :, half:] * factors[i] for i in range(n))
+        denom = sum(pltpu.roll(tops[i], LANES - count, 1) * factors[i] for i in range(n))
         for head in range(width // HD):
             cols = slice(head * HD, (head + 1) * HD)
             lane = slice(head, head + 1)
@@ -132,10 +135,10 @@
         outs[group, :, cols] = jnp.dot(
             weights.astype(BF16), v_ref[:, cols], preferred_element_type=F32
         ).astype(BF16)
-        side = jnp.where(lane == head, top, jnp.where(lane == head + half, total, side))
-    sides[group] = side
+        side = jnp.where(lane == head, top, jnp.where(lane == head + count, total, side))
+    sides[group] = side.T[: sides.shape[1], :]
     launch(scatter(group))
-    stats[group, me] = sides[group, mine, :]
+    stats[group, me] = sides[group]
     parts[group, me] = outs[group, mine, :]
 
     @pl.when(group > 0)
@@ -180,9 +183,10 @@
         out_shape=jax.ShapeDtypeStruct((rows, width), BF16),
         scratch_shapes=[
             pltpu.VMEM((groups, rows, part), BF16),
-            pltpu.VMEM((groups, rows, LANES), F32),
+            pltpu.VMEM((groups, 2 * HEADS_AT_ONCE, rows), F32),
             pltpu.VMEM((groups, n, rows // n, part), BF16),
-            pltpu.VMEM((groups, n, rows // n, LANES), F32),
+            pltpu.VMEM((groups, n, 2 * HEADS_AT_ONCE, rows), F32),
+            pltpu.VMEM((n, rows, LANES), F32),
             pltpu.VMEM((groups, rows, part), BF16),
         ]
         + [sem] * 6,
@@ -297,10 +301,12 @@
         return carry
 
     lax.fori_loop(0, SWEEPS, sweep, 0)
-    states[...] = low[...]
-    out_ref[me] = states[rows_of(me, block), :]
+    change = (low[...] - jnp.concatenate([start] * times, axis=0)).astype(BF16)
+    for i in range(n):
+        states[i] = change[i * block : (i + 1) * block, :]
+    out_ref[me] = states[me]
     for copy in launch(
-        spread("tm", lambda p: states.at[rows_of(p, block)], lambda m: out_ref.at[m], s3, r3)
+        spread("tm", lambda p: states.at[p], lambda m: out_ref.at[m], s3, r3)
     ):
         copy.wait()
 
@@ -311,14 +317,14 @@
     times, width = embedding.shape
     return pl.pallas_call(
         functools.partial(sweep_kernel, model_width),
-        out_shape=jax.ShapeDtypeStruct((n, times // n * each, chan), F32),
+        out_shape=jax.ShapeDtypeStruct((n, times // n * each, chan), BF16),
         in_specs=[VMEM] * 8,
         out_specs=VMEM,
         scratch_shapes=[
             pltpu.VMEM(cond.shape, F32),
             pltpu.VMEM(square.shape, F32),
             pltpu.VMEM((times * each, width), F32),
-            pltpu.VMEM((times * each, chan), F32),
+            pltpu.VMEM((n, times // n * each, chan), BF16),
             pltpu.VMEM((times * each, chan), F32),
             pltpu.VMEM((times * each, width), BF16),
         ]
@@ -383,7 +389,7 @@
     embedding, step_size, noise_scale = time_terms(plan.astype(F32), width)
     noise_term = noise.astype(F32).reshape(times, each, chan) * noise_scale[:, None, None]
     start = lax.dynamic_slice_in_dim(start_state, when * each, each, 0)
-    states = sweeps(
+    change = sweeps(
         model_width,
         cond,
         square.reshape(n, each, LANES),
@@ -394,8 +400,8 @@
         in_weight,
         head_out,
     )
-    states = states.reshape(n, time_each, each, chan).transpose(0, 2, 1, 3)
-    return states.reshape(row_each, time_each, chan)
+    change = change.reshape(n, time_each, each, chan).transpose(0, 2, 1, 3)
+    return start_state[:, None, :] + change.reshape(row_each, time_each, chan).astype(F32)
 
 
 def solution(mesh):

time: 112 us -> 106 us (0.946)
  Pallas kernels: 75.3 us -> 70 us
  local copies, waits for them, and re-layouts: 7.17 us -> 4.75 us
  other arithmetic: 4.88 us -> 6.73 us
    pallas_call x1, Pallas kernels: 26.4 us -> 23.1 us  [sweeps(): pl.pallas_call(functools.partial(sweep_kernel, model_width), out_shape=ja...]
    pallas_call x1, Pallas kernels: 39.1 us -> 36.9 us  [attend(): pl.pallas_call(attend_kernel, grid=(groups,), in_specs=[pl.BlockSpec(memo...]
    transpose x1 -> x0, local copies, waits for them, and re-layouts: 1.83 us -> none  [shards(): states = states.reshape(n, time_each, each, chan).transpose(0, 2, 1, 3)]
where the time goes in v3:
time: 106 us
  Pallas kernels  70 us (66%)
  between operations  14.1 us (13%)
  matrix products  9.66 us (9%)
  other arithmetic  6.73 us (6%)
  local copies, waits for them, and re-layouts  4.75 us (4%)
    pallas_call x1, Pallas kernels, attend(): pl.pallas_call(attend_kernel, grid=(groups,), in_specs=[pl.BlockSpec(memo...  36.9 us
    pallas_call x1, Pallas kernels, sweeps(): pl.pallas_call(functools.partial(sweep_kernel, model_width), out_shape=ja...  23.1 us
    pallas_call x1, Pallas kernels, hidden_rows(): pl.pallas_call(hidden_kernel, out_shape=[jax.ShapeDtypeStruct((each, widt...  9.94 us
    dot_general x1, matrix products, shards(): jnp.dot(attended, out_weight, preferred_element_type=F32).astype(BF16)  5.66 us
    dot_general x1, matrix products, shards(): jnp.einsum('rk,hkc->rhc', scaled, cond_all, preferred_element_type=F32)  3.99 us
  transfers between devices with their start and end apart: 1, of which 0 were waited for; matrix products, arithmetic and copies ran while one was open for 13% of the time, Pallas kernels for 44%

profile of v3, /device:TPU:0, one launch (start us, length us, event | category | flops | bytes accessed | tf_op | source)
XLA Modules:
  0.0 105.9 jit_solution(8453299084588083978)
XLA Ops:
  6.5 0.0 copy-start
  6.5 0.0 all-gather.3.cloned.1.call-start
  6.5 0.7 all-gather.3.cloned.1.call-update
  7.9 0.7 convert_element_type.29
  8.6 1.6 %copy.19 = bf16[4,8,2,1152]{3,1,2,0:T(8,128)(2,1)} copy(bf16[4,8,2,1152]{3,2,1,0:T(2,128)(2,1)} %bitcast.28) | data formatting | bytes 294912 | tf_op jit(solution)/shard_map/reshape | solution.py:382
  10.2 0.7 convert_element_type.32
  10.8 0.1 fusion.5
  10.9 0.1 mul.63
  11.0 0.1 mul.64
  11.1 1.0 multiply_sine_fusion
  12.0 36.9 %shard_map.136 = bf16[128,2048]{1,0:T(8,128)(2,1)} custom-call(s32[1]{0:T(128)S(6)} %sub.16.valid_ref, bf16[128,2048]{1,0:T(8,128)(2,1)} %q_ref.1, f32[128,128]{1,0:T(8,128)} %get-tuple-element.16.cos_ref, f32[128,128]{1,0:T(8,128)} %get-tuple-element.15.sin_ref, bf16[1024,2048]{1,0:T(8,128)(2,1)} %k_ref.1, bf16[1024,2048]{1,0:T(8,128)(2,1)} %v_ref.1), custom_call_target="tpu_custom_call" | custom-call | flops 1073741824 | bytes 8388608 | tf_op jit(solution)/shard_map/pallas_call | solution.py:175
  49.0 0.0 copy-done
  49.0 0.7 constant_dynamic-slice_fusion.1.res_ref
  49.6 0.0 copy-start.1
  49.6 5.7 %convolution_convert_fusion.part_ref = bf16[128,2048]{1,0:T(8,128)(2,1)} fusion(bf16[128,2048]{1,0:T(8,128)(2,1)} %shard_map.136, bf16[2048,2048]{1,0:T(8,128)(2,1)} %param.18), kind=kOutput, calls=%fused_computation | convolution fusion | flops 1074003968 | bytes 9437184 | tf_op jit(solution)/shard_map/dot_general | solution.py:380
  55.3 9.9 %shard_map.137 = (bf16[32,2048]{1,0:T(8,128)(2,1)}, f32[32,128]{1,0:T(8,128)}, bf16[4,16,1152]{2,1,0:T(8,128)(2,1)}) custom-call(bf16[128,2048]{1,0:T(8,128)(2,1)} %convolution_convert_fusion.part_ref, bf16[32,2048]{1,0:T(8,128)(2,1)} %constant_dynamic-slice_fusion.1.res_ref, f32[1,2048]{1,0:T(1,128)} %bitcast.30, bf16[4,16,1152]{2,1,0:T(8,128)(2,1)} %bitcast.27), custom_call_target="tpu_custom_call" | custom-call | tf_op jit(solution)/shard_map/pallas_call | solution.py:231
  65.3 0.2 multiply_sine_fusion.1
  65.4 0.0 copy-done.1
  65.4 0.6 constant_dynamic-slice_fusion.start_ref
  66.1 0.6 pad_maximum_fusion.emb_ref
  66.7 1.7 %convert_multiply_fusion.noise_ref = f32[64,1152]{1,0:T(8,128)} fusion(bf16[4,16,1152]{2,1,0:T(8,128)(2,1)} %get-tuple-element.10, f32[64]{0:T(128)S(1)} %mul.64), kind=kLoop, calls=%fused_computation.2 | loop fusion | flops 147456 | bytes 442624 | tf_op jit(solution)/shard_map/mul | solution.py:390
  68.4 0.0 all-gather.3.cloned.1.call-done
  68.4 4.0 %fusion = f32[32,4,384]{2,0,1:T(8,128)S(1)} fusion(bf16[4,2048,384]{2,1,0:T(8,128)(2,1)} %bitcast.26, bf16[32,2048]{1,0:T(8,128)(2,1)} %get-tuple-element.8), kind=kOutput, calls=%fused_computation.5 | convolution fusion | flops 201326592 | bytes 6619136 | tf_op jit(solution)/shard_map/rk,hkc->rhc/dot_general | solution.py:387
  72.4 0.1 copy.16
  72.6 0.7 reshape.55.cond_ref
  73.3 0.7 broadcast_in_dim.5.step_ref
  74.0 23.1 %shard_map.138 = bf16[4,16,1152]{2,1,0:T(8,128)(2,1)} custom-call(f32[4,8,1536]{2,1,0:T(8,128)} %reshape.55.cond_ref, f32[4,8,128]{2,1,0:T(8,128)} %bitcast.29, f32[8,1152]{1,0:T(8,128)} %constant_dynamic-slice_fusion.start_ref, f32[8,1536]{1,0:T(8,128)} %pad_maximum_fusion.emb_ref, f32[8,128]{1,0:T(8,128)} %broadcast_in_dim.5.step_ref, ...), custom_call_target="tpu_custom_call" | custom-call | tf_op jit(solution)/shard_map/pallas_call | solution.py:318
  97.1 0.9 convert_bitcast_fusion
  98.0 0.2 copy.17
  98.2 0.9 bitcast_add_fusion
  (2 shorter events, 0.0 us)
Async XLA Ops:
  6.5 42.4 %copy-start = (bf16[128,2048]{1,0:T(8,128)(2,1)S(1)}, bf16[128,2048]{1,0:T(8,128)(2,1)}, u32[]{:S(2)}) copy-start(bf16[128,2048]{1,0:T(8,128)(2,1)} %param.17) | copy-start | bytes 1572868
  6.5 61.9 %all-gather.3.cloned.1.call-start = ((), (), s32[]{:S(2)}) async-start(), calls=%async_computation | async-start | bytes 7864320 | tf_op jit(solution)/shard_map/all_gather | solution.py:371
  49.6 15.8 %copy-start.1 = (f32[32,1152]{1,0:T(8,128)S(1)}, f32[32,1152]{1,0:T(8,128)}, u32[]{:S(2)}) copy-start(f32[32,1152]{1,0:T(8,128)} %param.23) | copy-start | bytes 442372
Sparse Core Ops, SparseCore 0:
  8.9 49.0 all-gather.2

commit v4 on v3

--- a/solution.py
+++ b/solution.py
@@ -243,8 +243,9 @@
 
 
 def sweep_kernel(
-    model_width, cond_ref, square_ref, start_ref, emb_ref, step_ref, noise_ref, in_ref, head_ref,
-    out_ref, conds, squares, base, states, low, action, s1, r1, s2, r2, s3, r3,
+    model_width, cond_ref, square_ref, start_ref, emb_ref, step_ref, noise_ref, in_hbm, head_hbm,
+    out_ref, conds, squares, base, states, low, action, in_ref, head_ref, load,
+    s1, r1, s2, r2, s3, r3,
 ):
     n = lax.axis_size("tm")
     me = lax.axis_index("tm")
@@ -252,6 +253,12 @@
     width = emb_ref.shape[1]
     times = emb_ref.shape[0]
     block = times // n * each
+    loads = launch(
+        [
+            pltpu.make_async_copy(in_hbm, in_ref, load.at[0]),
+            pltpu.make_async_copy(head_hbm, head_ref, load.at[1]),
+        ]
+    )
     greet(["tm"])
     copies = launch(spread("tm", lambda p: cond_ref.at[p], lambda m: conds.at[m], s1, r1))
     copies += launch(
@@ -269,6 +276,8 @@
     condition = sum(conds[i] for i in range(n)) * inverse
     for j in range(times):
         base[j * each : (j + 1) * each, :] = condition + emb_ref[j : j + 1, :]
+    for copy in loads:
+        copy.wait()
     tile = 512 if width % 512 == 0 else width
     tile_out = 384 if chan % 384 == 0 else chan
 
@@ -318,7 +327,7 @@
     return pl.pallas_call(
         functools.partial(sweep_kernel, model_width),
         out_shape=jax.ShapeDtypeStruct((n, times // n * each, chan), BF16),
-        in_specs=[VMEM] * 8,
+        in_specs=[VMEM] * 6 + [pl.BlockSpec(memory_space=pl.ANY)] * 2,
         out_specs=VMEM,
         scratch_shapes=[
             pltpu.VMEM(cond.shape, F32),
@@ -327,6 +336,9 @@
             pltpu.VMEM((n, times // n * each, chan), BF16),
             pltpu.VMEM((times * each, chan), F32),
             pltpu.VMEM((times * each, width), BF16),
+            pltpu.VMEM(in_weight.shape, BF16),
+            pltpu.VMEM(head_out.shape, BF16),
+            pltpu.SemaphoreType.DMA((2,)),
         ]
         + sems("tm", "tm", "tm"),
         compiler_params=comm_params(3),

time: 106 us -> 104 us (0.981)
  Pallas kernels: 70 us -> 67.8 us
    pallas_call x1, Pallas kernels: 23.1 us -> 20.9 us  [sweeps(): pl.pallas_call(functools.partial(sweep_kernel, model_width), out_shape=ja...]
  transfers between devices with their start and end apart: 1 -> 1, of which waited for: 0 -> 0; matrix products, arithmetic and copies ran while one was open for 13% -> 13% of each run, Pallas kernels for 44% -> 45%
where the time goes in v4:
time: 104 us
  Pallas kernels  67.8 us (65%)
  between operations  14.1 us (14%)
  matrix products  9.66 us (9%)
  other arithmetic  6.73 us (6%)
  local copies, waits for them, and re-layouts  4.75 us (5%)
    pallas_call x1, Pallas kernels, attend(): pl.pallas_call(attend_kernel, grid=(groups,), in_specs=[pl.BlockSpec(memo...  36.9 us
    pallas_call x1, Pallas kernels, sweeps(): pl.pallas_call(functools.partial(sweep_kernel, model_width), out_shape=ja...  20.9 us
    pallas_call x1, Pallas kernels, hidden_rows(): pl.pallas_call(hidden_kernel, out_shape=[jax.ShapeDtypeStruct((each, widt...  9.94 us
    dot_general x1, matrix products, shards(): jnp.dot(attended, out_weight, preferred_element_type=F32).astype(BF16)  5.66 us
    dot_general x1, matrix products, shards(): jnp.einsum('rk,hkc->rhc', scaled, cond_all, preferred_element_type=F32)  3.99 us
  transfers between devices with their start and end apart: 1, of which 0 were waited for; matrix products, arithmetic and copies ran while one was open for 13% of the time, Pallas kernels for 45%

profile of v4, /device:TPU:0, one launch (start us, length us, event | category | flops | bytes accessed | tf_op | source)
XLA Modules:
  0.0 103.7 jit_solution(14852930529201348889)
XLA Ops:
  6.5 0.0 copy-start
  6.5 0.0 all-gather.3.cloned.1.call-start
  6.5 0.7 all-gather.3.cloned.1.call-update
  7.9 0.7 convert_element_type.29
  8.6 1.6 %copy.19 = bf16[4,8,2,1152]{3,1,2,0:T(8,128)(2,1)} copy(bf16[4,8,2,1152]{3,2,1,0:T(2,128)(2,1)} %bitcast.28) | data formatting | bytes 294912 | tf_op jit(solution)/shard_map/reshape | solution.py:394
  10.2 0.7 convert_element_type.32
  10.8 0.1 fusion.5
  10.9 0.1 mul.63
  11.0 0.1 mul.64
  11.1 1.0 multiply_sine_fusion
  12.0 36.9 %shard_map.136 = bf16[128,2048]{1,0:T(8,128)(2,1)} custom-call(s32[1]{0:T(128)S(6)} %sub.16.valid_ref, bf16[128,2048]{1,0:T(8,128)(2,1)} %q_ref.1, f32[128,128]{1,0:T(8,128)} %get-tuple-element.16.cos_ref, f32[128,128]{1,0:T(8,128)} %get-tuple-element.15.sin_ref, bf16[1024,2048]{1,0:T(8,128)(2,1)} %k_ref.1, bf16[1024,2048]{1,0:T(8,128)(2,1)} %v_ref.1), custom_call_target="tpu_custom_call" | custom-call | flops 1073741824 | bytes 8388608 | tf_op jit(solution)/shard_map/pallas_call | solution.py:175
  49.0 0.0 copy-done
  49.0 0.7 constant_dynamic-slice_fusion.1.res_ref
  49.6 0.0 copy-start.1
  49.6 5.7 %convolution_convert_fusion.part_ref = bf16[128,2048]{1,0:T(8,128)(2,1)} fusion(bf16[128,2048]{1,0:T(8,128)(2,1)} %shard_map.136, bf16[2048,2048]{1,0:T(8,128)(2,1)} %param.18), kind=kOutput, calls=%fused_computation | convolution fusion | flops 1074003968 | bytes 9437184 | tf_op jit(solution)/shard_map/dot_general | solution.py:392
  55.3 9.9 %shard_map.137 = (bf16[32,2048]{1,0:T(8,128)(2,1)}, f32[32,128]{1,0:T(8,128)}, bf16[4,16,1152]{2,1,0:T(8,128)(2,1)}) custom-call(bf16[128,2048]{1,0:T(8,128)(2,1)} %convolution_convert_fusion.part_ref, bf16[32,2048]{1,0:T(8,128)(2,1)} %constant_dynamic-slice_fusion.1.res_ref, f32[1,2048]{1,0:T(1,128)} %bitcast.30, bf16[4,16,1152]{2,1,0:T(8,128)(2,1)} %bitcast.27), custom_call_target="tpu_custom_call" | custom-call | tf_op jit(solution)/shard_map/pallas_call | solution.py:231
  65.3 0.2 multiply_sine_fusion.1
  65.4 0.0 copy-done.1
  65.4 0.6 constant_dynamic-slice_fusion.start_ref
  66.1 0.6 pad_maximum_fusion.emb_ref
  66.7 1.7 %convert_multiply_fusion.noise_ref = f32[64,1152]{1,0:T(8,128)} fusion(bf16[4,16,1152]{2,1,0:T(8,128)(2,1)} %get-tuple-element.10, f32[64]{0:T(128)S(1)} %mul.64), kind=kLoop, calls=%fused_computation.2 | loop fusion | flops 147456 | bytes 442624 | tf_op jit(solution)/shard_map/mul | solution.py:402
  68.4 0.0 all-gather.3.cloned.1.call-done
  68.4 4.0 %fusion = f32[32,4,384]{2,0,1:T(8,128)S(1)} fusion(bf16[4,2048,384]{2,1,0:T(8,128)(2,1)} %bitcast.26, bf16[32,2048]{1,0:T(8,128)(2,1)} %get-tuple-element.8), kind=kOutput, calls=%fused_computation.5 | convolution fusion | flops 201326592 | bytes 6619136 | tf_op jit(solution)/shard_map/rk,hkc->rhc/dot_general | solution.py:399
  72.4 0.1 copy.16
  72.6 0.7 reshape.55.cond_ref
  73.3 0.7 broadcast_in_dim.5.step_ref
  74.0 20.9 %shard_map.138 = bf16[4,16,1152]{2,1,0:T(8,128)(2,1)} custom-call(f32[4,8,1536]{2,1,0:T(8,128)} %reshape.55.cond_ref, f32[4,8,128]{2,1,0:T(8,128)} %bitcast.29, f32[8,1152]{1,0:T(8,128)} %constant_dynamic-slice_fusion.start_ref, f32[8,1536]{1,0:T(8,128)} %pad_maximum_fusion.emb_ref, f32[8,128]{1,0:T(8,128)} %broadcast_in_dim.5.step_ref, ...), custom_call_target="tpu_custom_call" | custom-call | tf_op jit(solution)/shard_map/pallas_call | solution.py:327
  94.9 0.9 convert_bitcast_fusion
  95.8 0.2 copy.17
  96.0 0.9 bitcast_add_fusion
  (2 shorter events, 0.0 us)
Async XLA Ops:
  6.5 42.4 %copy-start = (bf16[128,2048]{1,0:T(8,128)(2,1)S(1)}, bf16[128,2048]{1,0:T(8,128)(2,1)}, u32[]{:S(2)}) copy-start(bf16[128,2048]{1,0:T(8,128)(2,1)} %param.17) | copy-start | bytes 1572868
  6.5 61.9 %all-gather.3.cloned.1.call-start = ((), (), s32[]{:S(2)}) async-start(), calls=%async_computation | async-start | bytes 7864320 | tf_op jit(solution)/shard_map/all_gather | solution.py:383
  49.6 15.8 %copy-start.1 = (f32[32,1152]{1,0:T(8,128)S(1)}, f32[32,1152]{1,0:T(8,128)}, u32[]{:S(2)}) copy-start(f32[32,1152]{1,0:T(8,128)} %param.23) | copy-start | bytes 442372
Sparse Core Ops, SparseCore 0:
  8.9 49.0 all-gather.2

commit v5 on v4

--- a/solution.py
+++ b/solution.py
@@ -130,7 +130,7 @@
         ) * (1.0 / math.sqrt(HD))
         masked = jnp.where(valid, scores, F32(-1e30))
         top = jnp.max(masked, axis=1, keepdims=True)
-        weights = jnp.where(valid, jnp.exp(masked - top), F32(0.0))
+        weights = jnp.exp(masked - jnp.maximum(top, F32(-1e29)))
         total = jnp.sum(weights, axis=1, keepdims=True)
         outs[group, :, cols] = jnp.dot(
             weights.astype(BF16), v_ref[:, cols], preferred_element_type=F32

time: 104 us -> 104 us (level)
  no operation moved by 1% of the time
where the time goes in v5:
time: 104 us
  Pallas kernels  67.6 us (65%)
  between operations  14.1 us (14%)
  matrix products  9.66 us (9%)
  other arithmetic  6.73 us (6%)
  local copies, waits for them, and re-layouts  4.75 us (5%)
    pallas_call x1, Pallas kernels, attend(): pl.pallas_call(attend_kernel, grid=(groups,), in_specs=[pl.BlockSpec(memo...  36.9 us
    pallas_call x1, Pallas kernels, sweeps(): pl.pallas_call(functools.partial(sweep_kernel, model_width), out_shape=ja...  20.7 us
    pallas_call x1, Pallas kernels, hidden_rows(): pl.pallas_call(hidden_kernel, out_shape=[jax.ShapeDtypeStruct((each, widt...  10 us
    dot_general x1, matrix products, shards(): jnp.dot(attended, out_weight, preferred_element_type=F32).astype(BF16)  5.66 us
    dot_general x1, matrix products, shards(): jnp.einsum('rk,hkc->rhc', scaled, cond_all, preferred_element_type=F32)  3.99 us
  transfers between devices with their start and end apart: 1, of which 0 were waited for; matrix products, arithmetic and copies ran while one was open for 13% of the time, Pallas kernels for 45%

profile of v5, /device:TPU:0, one launch (start us, length us, event | category | flops | bytes accessed | tf_op | source)
XLA Modules:
  0.0 103.6 jit_solution(866012330448704171)
XLA Ops:
  6.5 0.0 copy-start
  6.5 0.0 all-gather.3.cloned.1.call-start
  6.5 0.7 all-gather.3.cloned.1.call-update
  7.9 0.7 convert_element_type.29
  8.6 1.6 %copy.19 = bf16[4,8,2,1152]{3,1,2,0:T(8,128)(2,1)} copy(bf16[4,8,2,1152]{3,2,1,0:T(2,128)(2,1)} %bitcast.28) | data formatting | bytes 294912 | tf_op jit(solution)/shard_map/reshape | solution.py:394
  10.2 0.7 convert_element_type.32
  10.8 0.1 fusion.5
  10.9 0.1 mul.63
  11.0 0.1 mul.64
  11.1 1.0 multiply_sine_fusion
  12.0 36.9 %shard_map.136 = bf16[128,2048]{1,0:T(8,128)(2,1)} custom-call(s32[1]{0:T(128)S(6)} %sub.16.valid_ref, bf16[128,2048]{1,0:T(8,128)(2,1)} %q_ref.1, f32[128,128]{1,0:T(8,128)} %get-tuple-element.16.cos_ref, f32[128,128]{1,0:T(8,128)} %get-tuple-element.15.sin_ref, bf16[1024,2048]{1,0:T(8,128)(2,1)} %k_ref.1, bf16[1024,2048]{1,0:T(8,128)(2,1)} %v_ref.1), custom_call_target="tpu_custom_call" | custom-call | flops 1073741824 | bytes 8388608 | tf_op jit(solution)/shard_map/pallas_call | solution.py:175
  48.9 0.0 copy-done
  48.9 0.7 constant_dynamic-slice_fusion.1.res_ref
  49.6 0.0 copy-start.1
  49.6 5.7 %convolution_convert_fusion.part_ref = bf16[128,2048]{1,0:T(8,128)(2,1)} fusion(bf16[128,2048]{1,0:T(8,128)(2,1)} %shard_map.136, bf16[2048,2048]{1,0:T(8,128)(2,1)} %param.18), kind=kOutput, calls=%fused_computation | convolution fusion | flops 1074003968 | bytes 9437184 | tf_op jit(solution)/shard_map/dot_general | solution.py:392
  55.3 10.0 %shard_map.137 = (bf16[32,2048]{1,0:T(8,128)(2,1)}, f32[32,128]{1,0:T(8,128)}, bf16[4,16,1152]{2,1,0:T(8,128)(2,1)}) custom-call(bf16[128,2048]{1,0:T(8,128)(2,1)} %convolution_convert_fusion.part_ref, bf16[32,2048]{1,0:T(8,128)(2,1)} %constant_dynamic-slice_fusion.1.res_ref, f32[1,2048]{1,0:T(1,128)} %bitcast.30, bf16[4,16,1152]{2,1,0:T(8,128)(2,1)} %bitcast.27), custom_call_target="tpu_custom_call" | custom-call | tf_op jit(solution)/shard_map/pallas_call | solution.py:231
  65.3 0.2 multiply_sine_fusion.1
  65.5 0.0 copy-done.1
  65.5 0.6 constant_dynamic-slice_fusion.start_ref
  66.1 0.6 pad_maximum_fusion.emb_ref
  66.8 1.7 %convert_multiply_fusion.noise_ref = f32[64,1152]{1,0:T(8,128)} fusion(bf16[4,16,1152]{2,1,0:T(8,128)(2,1)} %get-tuple-element.10, f32[64]{0:T(128)S(1)} %mul.64), kind=kLoop, calls=%fused_computation.2 | loop fusion | flops 147456 | bytes 442624 | tf_op jit(solution)/shard_map/mul | solution.py:402
  68.5 0.0 all-gather.3.cloned.1.call-done
  68.5 4.0 %fusion = f32[32,4,384]{2,0,1:T(8,128)S(1)} fusion(bf16[4,2048,384]{2,1,0:T(8,128)(2,1)} %bitcast.26, bf16[32,2048]{1,0:T(8,128)(2,1)} %get-tuple-element.8), kind=kOutput, calls=%fused_computation.5 | convolution fusion | flops 201326592 | bytes 6619136 | tf_op jit(solution)/shard_map/rk,hkc->rhc/dot_general | solution.py:399
  72.5 0.1 copy.16
  72.6 0.7 reshape.55.cond_ref
  73.4 0.7 broadcast_in_dim.5.step_ref
  74.0 20.7 %shard_map.138 = bf16[4,16,1152]{2,1,0:T(8,128)(2,1)} custom-call(f32[4,8,1536]{2,1,0:T(8,128)} %reshape.55.cond_ref, f32[4,8,128]{2,1,0:T(8,128)} %bitcast.29, f32[8,1152]{1,0:T(8,128)} %constant_dynamic-slice_fusion.start_ref, f32[8,1536]{1,0:T(8,128)} %pad_maximum_fusion.emb_ref, f32[8,128]{1,0:T(8,128)} %broadcast_in_dim.5.step_ref, ...), custom_call_target="tpu_custom_call" | custom-call | tf_op jit(solution)/shard_map/pallas_call | solution.py:327
  94.7 0.9 convert_bitcast_fusion
  95.7 0.2 copy.17
  95.8 0.9 bitcast_add_fusion
  (2 shorter events, 0.0 us)
Async XLA Ops:
  6.5 42.4 %copy-start = (bf16[128,2048]{1,0:T(8,128)(2,1)S(1)}, bf16[128,2048]{1,0:T(8,128)(2,1)}, u32[]{:S(2)}) copy-start(bf16[128,2048]{1,0:T(8,128)(2,1)} %param.17) | copy-start | bytes 1572868
  6.5 61.9 %all-gather.3.cloned.1.call-start = ((), (), s32[]{:S(2)}) async-start(), calls=%async_computation | async-start | bytes 7864320 | tf_op jit(solution)/shard_map/all_gather | solution.py:383
  49.6 15.9 %copy-start.1 = (f32[32,1152]{1,0:T(8,128)S(1)}, f32[32,1152]{1,0:T(8,128)}, u32[]{:S(2)}) copy-start(f32[32,1152]{1,0:T(8,128)} %param.23) | copy-start | bytes 442372
Sparse Core Ops, SparseCore 0:
  8.9 49.0 all-gather.2
